TPU v7x, 128 devices: a whole 4x4x4 slice. The times are simulated.
128 devices in a mesh: row: 16 (over y, x_lo, core), col: 8 (over z, x_hi).
Axes of the slice: x: 4 (x_hi: 2, x_lo: 2; x = x_hi * 2 + x_lo), y: 4, z: 4, core: 2. Of those that a mesh axis runs over, the one named last changes fastest.
Arguments:
- band_blocks: bfloat16 [256, 5, 512, 512], P(('row', 'col')), as said below
- occupancy: int32 [256, 5], P(('row', 'col')), may hold values from 0 to 1, as said below
Outputs:
- next_iterate: bfloat16 [256, 5, 512, 512], P(('row', 'col'))
Inputs may be any that keep to these rules, and one draw needn't show every extreme that they name: `band_blocks`: the matrix is symmetric: the block in block row i and block column j is the transpose of the block in block row j and block column i. `occupancy`: the pattern is symmetric and every diagonal block is occupied.
All inputs are finite; a program needn't handle non-finite values.
Results may differ from a plain program's by a relative error of at most 0.0038.
Values may be sent and summed in bfloat16 or wider, within the bound.
A program may use at most 128 MiB of HBM per device.

v0:
```python
import jax
import jax.numpy as jnp
from jax import lax
from jax.sharding import PartitionSpec as P

W = 2


def extended_2(block, sides, width):
    for axis, dim in sides:
        count = lax.axis_size(axis)
        forward = [(i, i + 1) for i in range(count - 1)]
        forward.append((count - 1, 0))
        backward = [(target, source) for source, target in forward]
        low = lax.ppermute(
            lax.slice_in_dim(block, block.shape[dim] - width, None, axis=dim), axis, forward
        )
        high = lax.ppermute(lax.slice_in_dim(block, 0, width, axis=dim), axis, backward)
        block = jnp.concatenate([low, block, high], axis=dim)
    return block


def banded_product(left_band, extended, keep_float):
    own_rows = left_band.shape[0]
    slot_count = left_band.shape[1]
    half_width = (slot_count - 1) // 2
    running = jnp.zeros(left_band.shape, jnp.float32)
    for left_slot in range(slot_count):
        first_out = max(0, left_slot - half_width)
        last_out = min(slot_count - 1, left_slot + half_width)
        neighbours = extended[
            left_slot : left_slot + own_rows,
            first_out - left_slot + half_width : last_out - left_slot + half_width + 1,
        ]
        contribution = jnp.einsum(
            "iqc,iscb->isqb",
            left_band[:, left_slot],
            neighbours,
            preferred_element_type=jnp.float32,
        )
        running = running.at[:, first_out : last_out + 1].add(contribution)
    return running * keep_float[:, :, None, None]


def on_device(band_blocks, occupancy):
    keep_float = occupancy.astype(jnp.float32)
    masked = band_blocks * occupancy.astype(jnp.bfloat16)[:, :, None, None]
    extended = extended_2(masked, ((("row", "col"), 0),), W)
    square = banded_product(masked, extended, keep_float).astype(jnp.bfloat16)
    cubic = banded_product(square, extended, keep_float)
    factor = 0.5 / (band_blocks.shape[1] * band_blocks.shape[3])
    return (1.5 * masked.astype(jnp.float32) - factor * cubic).astype(jnp.bfloat16)


def solution(mesh):
    return jax.shard_map(
        on_device,
        mesh=mesh,
        in_specs=(P(("row", "col"), None, None, None), P(("row", "col"), None)),
        out_specs=P(("row", "col"), None, None, None),
        check_vma=False,
    )
```

profile of v0, /device:TPU:0, one launch (start us, length us, event | category | flops | bytes accessed | tf_op | source)
XLA Modules:
  0.0 338.7 jit_solution(10344556663558572866)
XLA Ops:
  0.0 0.8 fusion.22
  0.8 0.1 copy.3
  0.9 5.3 %copy_multiply_fusion = bf16[2,5,512,512]{3,2,0,1:T(8,128)(2,1)} fusion(bf16[2,5,512,512]{3,2,1,0:T(8,128)(2,1)} %param.26, bf16[2,5]{0,1:T(8,128)(2,1)S(1)} %copy.3), kind=kLoop, calls=%fused_computation.14 | loop fusion | flops 2621440 | bytes 10485780 | tf_op jit(solution)/shard_map/mul | solution.py:47
  6.1 3.1 collective-permute-start
  9.2 5.1 %collective-permute-start.1 = (bf16[2,5,512,512]{3,2,0,1:T(8,128)(2,1)}, bf16[2,5,512,512]{3,2,0,1:T(8,128)(2,1)}, u32[]{:S(2)}, u32[]{:S(2)}) collective-permute-start(bf16[2,5,512,512]{3,2,0,1:T(8,128)(2,1)} %copy_multiply_fusion), channel_id=1, source_target_pairs={{1,0},{2,1},{3,2},{4,3},{5,4},{6,5},{7,6},{8,7},{9,8},{10,9},{11,1... | collective-permute-start | bytes 15728648 | tf_op jit(solution)/shard_map/ppermute | solution.py:18
  14.3 0.1 copy.15
  14.4 226.2 %collective-permute-done = bf16[2,5,512,512]{3,2,0,1:T(8,128)(2,1)} collective-permute-done((bf16[2,5,512,512]{3,2,0,1:T(8,128)(2,1)}, bf16[2,5,512,512]{3,2,0,1:T(8,128)(2,1)}, u32[]{:S(2)}, u32[]{:S(2)}) %collective-permute-start) | collective-permute-done | bytes 5242912 | tf_op jit(solution)/shard_map/ppermute | solution.py:15
  240.6 4.0 %fusion.15 = f32[2,3,512,512]{3,2,0,1:T(8,128)S(1)} fusion(bf16[2,5,512,512]{3,2,0,1:T(8,128)(2,1)} %collective-permute-done, bf16[2,5,512,512]{3,2,0,1:T(8,128)(2,1)} %copy_multiply_fusion), kind=kOutput, calls=%fused_computation.26 | convolution fusion | flops 1610612736 | bytes 10485760 | tf_op jit(solution)/shard_map/iqc,iscb->isqb/dot_general | solution.py:35
  244.6 5.2 %scatter-add.26 = f32[2,5,512,512]{3,2,0,1:T(8,128)} pad(f32[2,3,512,512]{3,2,0,1:T(8,128)S(1)} %fusion.15, f32[]{:T(128)} %constant.251.clone.1), padding=0_0x0_2x0_0x0_0 | pad | bytes 16777220 | tf_op jit(solution)/shard_map/scatter-add | solution.py:41
  249.8 10.6 %fusion.1 = f32[2,5,512,512]{3,2,0,1:T(8,128)} fusion(f32[2,5,512,512]{3,2,0,1:T(8,128)} %scatter-add.26, bf16[2,5,512,512]{3,2,0,1:T(8,128)(2,1)} %copy_multiply_fusion, bf16[2,5,512,512]{3,2,0,1:T(8,128)(2,1)} %collective-permute-done), kind=kOutput, calls=%fused_computation.9 | convolution fusion | flops 2157969408 | bytes 28311552 | tf_op jit(solution)/shard_map/iqc,iscb->isqb/dot_general | solution.py:35
  260.4 8.7 %bitcast_add_fusion.1 = f32[2,5,512,512]{3,2,0,1:T(8,128)S(1)} fusion(f32[2,5,512,512]{3,2,0,1:T(8,128)} %fusion.1, bf16[2,5,512,512]{3,2,0,1:T(8,128)(2,1)} %copy_multiply_fusion), kind=kOutput, calls=%fused_computation.1 | convolution fusion | flops 2686976000 | bytes 27262976 | tf_op jit(solution)/shard_map/iqc,iscb->isqb/dot_general | solution.py:35
  269.1 0.0 collective-permute-done.1
  269.2 8.2 %constant_dynamic-update-slice_fusion.1 = (f32[2,5,512,512]{3,2,0,1:T(8,128)S(1)}, f32[2,4,512,512]{3,2,0,1:T(8,128)}) fusion(f32[2,5,512,512]{3,2,0,1:T(8,128)S(1)} %bitcast_add_fusion.1, bf16[2,5,512,512]{3,2,0,1:T(8,128)(2,1)} %collective-permute-done.1, bf16[2,5,512,512]{3,2,0,1:T(8,128)(2,1)} %copy_multiply_fusion), kind=kOutput, calls=%fused_computation.38 | convolution fusion | flops 2157969408 | bytes 36700160 | tf_op jit(solution)/shard_map/iqc,iscb->isqb/dot_general | solution.py:35
  277.3 5.9 %fusion.3 = f32[2,5,512,512]{3,2,0,1:T(8,128)S(1)} fusion(f32[2,5,512,512]{3,2,0,1:T(8,128)S(1)} %get-tuple-element.143, f32[2,4,512,512]{3,2,0,1:T(8,128)} %get-tuple-element.144, bf16[2,5,512,512]{3,2,0,1:T(8,128)(2,1)} %collective-permute-done.1, bf16[2,5,512,512]{3,2,0,1:T(8,128)(2,1)} %copy_multiply_fusion), kind=kOutput, calls=%fused_computation.13 | convolution fusion | flops 1612185600 | bytes 16777216 | tf_op jit(solution)/shard_map/iqc,iscb->isqb/dot_general | solution.py:35
  283.2 3.9 %multiply_convert_fusion = bf16[2,5,512,512]{3,2,0,1:T(8,128)(2,1)} fusion(f32[2,5,512,512]{3,2,0,1:T(8,128)S(1)} %fusion.3, f32[2,5]{0,1:T(8,128)S(1)} %copy.15), kind=kLoop, calls=%fused_computation.3 | loop fusion | flops 5242880 | bytes 15728680 | tf_op jit(solution)/shard_map/convert_element_type | solution.py:49
  287.1 4.2 %fusion.12 = f32[2,3,512,512]{3,2,0,1:T(8,128)S(1)} fusion(bf16[2,5,512,512]{3,2,0,1:T(8,128)(2,1)} %collective-permute-done, bf16[2,5,512,512]{3,2,0,1:T(8,128)(2,1)} %multiply_convert_fusion), kind=kOutput, calls=%fused_computation.25 | convolution fusion | flops 1610612736 | bytes 10485760 | tf_op jit(solution)/shard_map/iqc,iscb->isqb/dot_general | solution.py:35
  291.2 0.0 slice-start.1
  291.2 1.8 scatter-add.34
  293.1 5.3 %fusion = f32[2,5,512,512]{3,2,0,1:T(8,128)S(1)} fusion(f32[2,5,512,512]{3,2,0,1:T(8,128)S(1)} %scatter-add.34, bf16[2,5,512,512]{3,2,0,1:T(8,128)(2,1)S(1)} %bitcast.71, bf16[2,5,512,512]{3,2,0,1:T(8,128)(2,1)} %copy_multiply_fusion, bf16[2,5,512,512]{3,2,0,1:T(8,128)(2,1)} %collective-permute-done), kind=kOutput, calls=%fused_computation.7 | convolution fusion | flops 2157969408 | bytes 28311552 | tf_op jit(solution)/shard_map/iqc,iscb->isqb/dot_general | solution.py:35
  298.4 8.1 %bitcast_add_fusion = f32[2,5,512,512]{3,2,0,1:T(8,128)} fusion(f32[2,5,512,512]{3,2,0,1:T(8,128)S(1)} %fusion, bf16[2,5,512,512]{3,2,0,1:T(8,128)(2,1)} %copy_multiply_fusion, bf16[2,5,512,512]{3,2,0,1:T(8,128)(2,1)S(1)} %bitcast.71), kind=kOutput, calls=%fused_computation | convolution fusion | flops 2686976000 | bytes 27262976 | tf_op jit(solution)/shard_map/iqc,iscb->isqb/dot_general | solution.py:35
  306.5 10.5 %constant_dynamic-update-slice_fusion = (f32[2,5,512,512]{3,2,0,1:T(8,128)}, f32[2,4,512,512]{3,2,0,1:T(8,128)S(1)}) fusion(f32[2,5,512,512]{3,2,0,1:T(8,128)} %bitcast_add_fusion, bf16[2,5,512,512]{3,2,0,1:T(8,128)(2,1)} %collective-permute-done.1, bf16[2,5,512,512]{3,2,0,1:T(8,128)(2,1)} %copy_multiply_fusion, bf16[2,5,512,512]{3,2,0,1:T(8,128)(2,1)S(1)} %bitcast.71), kind=kOutput, calls=%fused_computation.37 | convolution fusion | flops 2157969408 | bytes 36700160 | tf_op jit(solution)/shard_map/iqc,iscb->isqb/dot_general | solution.py:35
  317.0 6.4 %fusion.2 = f32[2,5,512,512]{3,2,0,1:T(8,128)} fusion(f32[2,5,512,512]{3,2,0,1:T(8,128)} %get-tuple-element.145, f32[2,4,512,512]{3,2,0,1:T(8,128)S(1)} %get-tuple-element.146, bf16[2,5,512,512]{3,2,0,1:T(8,128)(2,1)} %collective-permute-done.1, bf16[2,5,512,512]{3,2,0,1:T(8,128)(2,1)S(1)} %bitcast.71), kind=kOutput, calls=%fused_computation.11 | convolution fusion | flops 1612185600 | bytes 16777216 | tf_op jit(solution)/shard_map/iqc,iscb->isqb/dot_general | solution.py:35
  323.4 10.1 %subtract_convert_fusion = bf16[2,5,512,512]{3,2,0,1:T(8,128)(2,1)} fusion(f32[2,5,512,512]{3,2,0,1:T(8,128)} %fusion.2, f32[2,5]{0,1:T(8,128)S(1)} %copy.15, bf16[2,5]{0,1:T(8,128)(2,1)S(1)} %copy.3, bf16[2,5,512,512]{3,2,1,0:T(8,128)(2,1)} %param.26), kind=kLoop, calls=%fused_computation.2 | loop fusion | flops 18350080 | bytes 20971580 | tf_op jit(solution)/shard_map/convert_element_type | solution.py:52
  333.5 5.2 %copy.26 = bf16[2,5,512,512]{3,2,1,0:T(8,128)(2,1)} copy(bf16[2,5,512,512]{3,2,0,1:T(8,128)(2,1)} %subtract_convert_fusion) | data formatting | bytes 10485760 | tf_op jit(solution)/shard_map/convert_element_type | solution.py:52
  (4 shorter events, 0.0 us)
Async XLA Ops:
  6.1 234.5 %collective-permute-start = (bf16[2,5,512,512]{3,2,0,1:T(8,128)(2,1)}, bf16[2,5,512,512]{3,2,0,1:T(8,128)(2,1)}, u32[]{:S(2)}, u32[]{:S(2)}) collective-permute-start(bf16[2,5,512,512]{3,2,0,1:T(8,128)(2,1)} %copy_multiply_fusion), channel_id=1, source_target_pairs={{0,1},{1,2},{2,3},{3,4},{4,5},{5,6},{6,7},{7,8},{8,9},{9,10},{10,1... | collective-permute-start | bytes 15728648 | tf_op jit(solution)/shard_map/ppermute | solution.py:15
  9.2 259.9 %collective-permute-start.1 = (bf16[2,5,512,512]{3,2,0,1:T(8,128)(2,1)}, bf16[2,5,512,512]{3,2,0,1:T(8,128)(2,1)}, u32[]{:S(2)}, u32[]{:S(2)}) collective-permute-start(bf16[2,5,512,512]{3,2,0,1:T(8,128)(2,1)} %copy_multiply_fusion), channel_id=1, source_target_pairs={{1,0},{2,1},{3,2},{4,3},{5,4},{6,5},{7,6},{8,7},{9,8},{10,9},{11,1... | collective-permute-start | bytes 15728648 | tf_op jit(solution)/shard_map/ppermute | solution.py:18
  287.1 6.0 %slice-start = ((s8[5242880]{0:T(1024)(128)(4,1)}), s8[4194304]{0:T(1024)(128)(4,1)S(1)}, s32[]{:S(2)}) async-start(s8[5242880]{0:T(1024)(128)(4,1)} %bitcast.70), calls=%async_computation | async-start | bytes 8388608
  291.2 1.9 slice-start.1
where the time goes:
time: 339 us
  waiting for transfers between devices  226 us (67%)
  matrix products  71.7 us (21%)
  other arithmetic  20 us (6%)
  local copies, waits for them, and re-layouts  12.5 us (4%)
  starting transfers between devices  8.21 us (2%)
    ppermute x1, waiting for transfers between devices, extended_2(): lax.ppermute(lax.slice_in_dim(block, block.shape[dim] - width, None, axis...  226 us
    dot_general x10, matrix products, banded_product(): jnp.einsum('iqc,iscb->isqb', left_band[:, left_slot], neighbours, preferr...  71.7 us
    convert_element_type x1, other arithmetic, on_device(): (1.5 * masked.astype(jnp.float32) - factor * cubic).astype(jnp.bfloat16)  10.1 us
    scatter-add x2, local copies, waits for them, and re-layouts, banded_product(): running = running.at[:, first_out:last_out + 1].add(contribution)  7.07 us
  transfers between devices with their start and end apart: 2, of which 1 were waited for; matrix products, arithmetic and copies ran while one was open for 8% of the time, Pallas kernels for 0%

commit v1 on v0

v1 whole, which is shorter than its diff:
```python
import jax
import jax.numpy as jnp
from jax import lax
from jax.experimental import pallas as pl
from jax.experimental.pallas import tpu as pltpu
from jax.sharding import PartitionSpec as P

F32, BF16 = jnp.float32, jnp.bfloat16
MESH = pl.DeviceIdType.MESH
B = 512
H = B // 2
OWN = 2
SLOTS = 5
SPAN = 6
MIB = 2**20


def chain(step):
    rows, cols = lax.axis_size("row"), lax.axis_size("col")
    place = lax.axis_index("row") * cols + lax.axis_index("col")
    other = lax.rem(place + (step + rows * cols), rows * cols)
    return {"row": lax.div(other, cols), "col": lax.rem(other, cols)}


def at(ref, row, col, height=1, width=1):
    return ref.at[row * B : (row + height) * B, col * B : (col + width) * B]


def product(left, right):
    return jnp.dot(left, right, preferred_element_type=F32)


def triangles():
    row = lax.broadcasted_iota(jnp.int32, (H, H), 0)
    col = lax.broadcasted_iota(jnp.int32, (H, H), 1)
    return row, col


def pack(first, second):
    row, col = triangles()
    first, second = first.astype(F32), second.astype(F32)
    tile = jnp.where(row <= col, first, second).astype(BF16)
    diagonal = jnp.sum(jnp.where(row == col, second, 0.0), axis=0, keepdims=True)
    return tile, diagonal


def unpack(tile, diagonal):
    row, col = triangles()
    tile = tile.astype(F32)
    turned = tile.T
    first = jnp.where(row <= col, tile, turned)
    second = jnp.where(row > col, tile, jnp.where(row < col, turned, diagonal))
    return first.astype(BF16), second.astype(BF16)


def halves(body):
    def step(n, carry):
        body(pl.multiple_of(n * H, H))
        return carry

    lax.fori_loop(0, 2, step, 0)


def kernel(
    band, occupancy, out,
    x, s, total, partial, done, send0, send1, low0, low1, high0, high1,
    load_sem, store_sem, send_sem, recv_sem,
):
    after, before = chain(1), chain(-1)
    barrier = pltpu.get_barrier_semaphore()
    for neighbour in (after, before):
        pl.semaphore_signal(barrier, inc=1, device_id=neighbour, device_id_type=MESH)

    def keep(row, col):
        return occupancy[row - OWN, col - (row - OWN)].astype(F32)

    own = [(row, col) for row in (2, 3) for col in range(row - 2, row + 3)]
    first = [(2, 3), (2, 2), (3, 3)]
    order = first + [pair for pair in own if pair not in first]
    loads = {}
    for n, (row, col) in enumerate(order):
        loads[row, col] = pltpu.make_async_copy(
            band.at[row - 2, col - (row - 2)], at(x, row, col), load_sem.at[n]
        )
        loads[row, col].start()

    def loaded(row, col):
        loads[row, col].wait()
        block = at(x, row, col)
        block[...] = (block[...].astype(F32) * keep(row, col)).astype(BF16)

    def send(piece, source, to_after, to_before):
        copies = []
        for side, (target, landing) in enumerate(((after, to_after), (before, to_before))):
            copy = pltpu.make_async_remote_copy(
                src_ref=source,
                dst_ref=landing,
                send_sem=send_sem.at[side, piece],
                recv_sem=recv_sem.at[side, piece],
                device_id=target,
                device_id_type=MESH,
            )
            copy.start()
            copies.append(copy)
        return copies

    loaded(2, 3)
    pl.semaphore_wait(barrier, 2)
    sent_a = send(0, at(x, 2, 3), at(x, 0, 1), at(x, 4, 5))
    loaded(2, 2)
    loaded(3, 3)
    a, b = at(x, 2, 2), at(x, 3, 3)
    tile, diagonal0 = pack(a[:H, :H], b[:H, :H])
    send0[:H, :H] = tile
    tile, diagonal1 = pack(a[H:, H:], b[H:, H:])
    send1[...] = tile
    send0[:H, H : 2 * H] = a[:H, H:]
    send0[:H, 2 * H :] = b[:H, H:]
    diagonals = jnp.concatenate([diagonal0, diagonal1, jnp.zeros((1, H), F32)], axis=1)
    send0[H:, :] = jnp.broadcast_to(diagonals, (16, 3 * H)).astype(BF16)
    sent_0 = send(1, send0, low0, high0)
    sent_1 = send(2, send1, low1, high1)

    for pair in order[3:]:
        loaded(*pair)
    for row, col in ((2, 0), (2, 1), (3, 1), (2, 4), (3, 4), (3, 5)):
        at(x, col, row)[...] = at(x, row, col)[...].T

    def square(row, col, low, high, scale):
        left = x[row * B : (row + 1) * B, low * B : high * B]

        def body(c):
            right = x[low * B : high * B, pl.ds(col * B + c, H)]
            value = product(left, right) * scale
            s[(row - 2) * B : (row - 1) * B, pl.ds(col * B + c, H)] = value.astype(BF16)

        halves(body)

    square(2, 2, 0, 5, keep(2, 2))
    square(3, 3, 1, 6, keep(3, 3))
    square(2, 3, 1, 5, keep(2, 3))
    at(s, 1, 2)[...] = at(s, 0, 3)[...].T

    def begin(row, col, low, high):
        left = s[(row - 2) * B : (row - 1) * B, low * B : high * B]

        def body(c):
            right = x[low * B : high * B, pl.ds(col * B + c, H)]
            total[(row - 2) * B : (row - 1) * B, pl.ds(col * B + c, H)] = product(left, right)

        halves(body)

    for row, col in own:
        begin(row, col, max(2, col - 2), min(4, col + 3))

    def part(n, row, col, low, high):
        left = x[row * B : (row + 1) * B, low * B : high * B]

        def body(c):
            right = x[low * B : high * B, pl.ds(col * B + c, H)]
            partial[:, pl.ds(n * B + c, H)] = product(left, right)

        halves(body)

    part(0, 2, 4, 2, 4)
    part(1, 3, 4, 2, 4)
    part(2, 3, 5, 3, 4)

    def unpack_a(corner):
        at(x, corner + 1, corner)[...] = at(x, corner, corner + 1)[...].T

    def unpack_0(corner, piece):
        upper, lower = unpack(piece[:H, :H], piece[H : H + 1, :H].astype(F32))
        for n, tile in enumerate((upper, lower)):
            base = (corner + n) * B
            x[base : base + H, base : base + H] = tile
            side = piece[:H, (n + 1) * H : (n + 2) * H]
            x[base : base + H, base + H : base + B] = side
            x[base + H : base + B, base : base + H] = side.T

    def unpack_1(corner, piece, first_piece):
        upper, lower = unpack(piece[...], first_piece[H : H + 1, H : 2 * H].astype(F32))
        for n, tile in enumerate((upper, lower)):
            base = (corner + n) * B
            x[base + H : base + B, base + H : base + B] = tile

    def finish(row, col):
        scale = keep(row, col) / (2.0 * SLOTS * B)
        block = 1.5 * at(x, row, col)[...].astype(F32) - scale * at(total, row - 2, col)[...]
        done[row - 2, col - (row - 2)] = block.astype(BF16)

    stores = []

    def store(row, col):
        copy = pltpu.make_async_copy(
            done.at[row - 2, col - (row - 2)], out.at[row - 2, col - (row - 2)], store_sem.at[row - 2, col - (row - 2)]
        )
        copy.start()
        stores.append(copy)

    sent_a[0].wait_recv()
    unpack_a(0)
    sent_0[0].wait_recv()
    unpack_0(0, low0)
    sent_1[0].wait_recv()
    unpack_1(0, low1, low0)
    square(2, 0, 0, 3, keep(2, 0))
    square(2, 1, 0, 4, keep(2, 1))
    square(3, 1, 1, 4, keep(3, 1))

    def add(row, col, low, high):
        left = s[(row - 2) * B : (row - 1) * B, low * B : high * B]

        def body(c):
            right = x[low * B : high * B, pl.ds(col * B + c, H)]
            total[(row - 2) * B : (row - 1) * B, pl.ds(col * B + c, H)] += product(left, right)

        halves(body)

    add(2, 0, 0, 2)
    add(2, 1, 0, 2)
    add(2, 2, 0, 2)
    add(2, 3, 1, 2)
    add(3, 1, 1, 2)
    add(3, 2, 1, 2)
    add(3, 3, 1, 2)
    for pair in ((2, 0), (2, 1), (3, 1)):
        finish(*pair)
        store(*pair)

    def square_high(c):
        scale = keep(2, 4)
        value = partial[:, c : c + H] + product(x[2 * B : 3 * B, 4 * B : 5 * B], x[4 * B : 5 * B, 4 * B + c : 4 * B + c + H])
        s[:B, 4 * B + c : 4 * B + c + H] = (value * scale).astype(BF16)
        for n in (0, 1):
            scale = keep(3, 4 + n)
            begin_col = (4 + n) * B + c
            value = partial[:, (n + 1) * B + c : (n + 1) * B + c + H]
            value += product(x[3 * B : 4 * B, 4 * B : 6 * B], x[4 * B : 6 * B, begin_col : begin_col + H])
            s[B:, begin_col : begin_col + H] = (value * scale).astype(BF16)

    def add_high(c, row, col):
        values = []
        blocks = [4] if row == 2 or col == 2 else [4, 5]
        for k in blocks:
            left = s[(row - 2) * B : (row - 1) * B, k * B + c : k * B + c + H]
            values.append(product(left, x[k * B + c : k * B + c + H, col * B : (col + 1) * B]))
        at(total, row - 2, col)[...] += sum(values[1:], values[0])

    touched = [(2, 2), (2, 3), (2, 4), (3, 2), (3, 3), (3, 4), (3, 5)]
    sent_a[1].wait_recv()
    unpack_a(4)
    sent_0[1].wait_recv()
    unpack_0(4, high0)
    square_high(0)
    for pair in touched:
        add_high(0, *pair)
    sent_1[1].wait_recv()
    unpack_1(4, high1, high0)
    square_high(H)
    for pair in touched:
        add_high(H, *pair)
        finish(*pair)
        store(*pair)
    for copies in (sent_a, sent_0, sent_1):
        for copy in copies:
            copy.wait_send()
    for copy in stores:
        copy.wait()


def on_device(band_blocks, occupancy):
    dma = pltpu.SemaphoreType.DMA
    return pl.pallas_call(
        kernel,
        out_shape=jax.ShapeDtypeStruct(band_blocks.shape, BF16),
        in_specs=[pl.BlockSpec(memory_space=pl.ANY), pl.BlockSpec(memory_space=pltpu.SMEM)],
        out_specs=pl.BlockSpec(memory_space=pl.ANY),
        scratch_shapes=[
            pltpu.VMEM((SPAN * B, SPAN * B), BF16),
            pltpu.VMEM((OWN * B, SPAN * B), BF16),
            pltpu.VMEM((OWN * B, SPAN * B), F32),
            pltpu.VMEM((B, 3 * B), F32),
            pltpu.VMEM((OWN, SLOTS, B, B), BF16),
            pltpu.VMEM((H + 16, 3 * H), BF16),
            pltpu.VMEM((H, H), BF16),
            pltpu.VMEM((H + 16, 3 * H), BF16),
            pltpu.VMEM((H, H), BF16),
            pltpu.VMEM((H + 16, 3 * H), BF16),
            pltpu.VMEM((H, H), BF16),
            dma((OWN * SLOTS,)),
            dma((OWN, SLOTS)),
            dma((2, 3)),
            dma((2, 3)),
        ],
        compiler_params=pltpu.CompilerParams(
            collective_id=0, has_side_effects=True, vmem_limit_bytes=60 * MIB
        ),
        name="step",
    )(band_blocks, occupancy)


def solution(mesh):
    return jax.shard_map(
        on_device,
        mesh=mesh,
        in_specs=(P(("row", "col"), None, None, None), P(("row", "col"), None)),
        out_specs=P(("row", "col"), None, None, None),
        check_vma=False,
    )
```

time: 339 us -> 78.7 us (0.23)
  waiting for transfers between devices: 226 us -> 0 us
  Pallas kernels: 0 us -> 73.4 us
  matrix products: 71.7 us -> 0 us
  other arithmetic: 20 us -> 0 us
  starting transfers between devices: 8.21 us -> 0 us
  local copies, waits for them, and re-layouts: 12.5 us -> 5.18 us
    ppermute x2 -> x0, waiting for transfers between devices: 226 us -> none  [the longest x1 226 us: extended_2(): lax.ppermute(lax.slice_in_dim(block, block.shape[dim] - width, None, axis...]
    pallas_call x0 -> x1, Pallas kernels: none -> 73.4 us  [on_device(): pl.pallas_call(kernel, out_shape=jax.ShapeDtypeStruct(band_blocks.shape,...]
    dot_general x10 -> x0, matrix products: 71.7 us -> none  [banded_product(): jnp.einsum('iqc,iscb->isqb', left_band[:, left_slot], neighbours, preferr...]
    convert_element_type x3 -> x0, other arithmetic: 14.8 us -> none  [the longest x1 10.1 us: on_device(): (1.5 * masked.astype(jnp.float32) - factor * cubic).astype(jnp.bfloat16)]
    ppermute x2 -> x0, starting transfers between devices: 8.21 us -> none  [the longest x1 5.1 us: extended_2(): lax.ppermute(lax.slice_in_dim(block, 0, width, axis=dim), axis, backward)]
    scatter-add x2 -> x0, local copies, waits for them, and re-layouts: 7.07 us -> none  [banded_product(): running = running.at[:, first_out:last_out + 1].add(contribution)]
    convert_element_type x3 -> x0, local copies, waits for them, and re-layouts: 5.38 us -> none  [the longest x1 5.18 us: on_device(): (1.5 * masked.astype(jnp.float32) - factor * cubic).astype(jnp.bfloat16)]
    mul x1 -> x0, other arithmetic: 5.25 us -> none  [on_device(): masked = band_blocks * occupancy.astype(jnp.bfloat16)[:, :, None, None]]
  transfers between devices with their start and end apart: 2 -> 0, of which waited for: 1 -> 0; matrix products, arithmetic and copies ran while one was open for 8% -> 0% of each run, Pallas kernels for 0% -> 0%
where the time goes in v1:
time: 78.7 us; the launch traced here: 78.6 us
  Pallas kernels  73.4 us (93%)
  local copies, waits for them, and re-layouts  5.18 us (7%)
    pallas_call x1, Pallas kernels, on_device(): pl.pallas_call(kernel, out_shape=jax.ShapeDtypeStruct(band_blocks.shape,...  73.4 us
    unnamed x1, local copies, waits for them, and re-layouts  5.18 us

profile of v1, /device:TPU:0, one launch (start us, length us, event | category | flops | bytes accessed | tf_op | source)
XLA Modules:
  0.0 78.6 jit_solution(4240161357543162569)
XLA Ops:
  0.0 73.4 %step.1 = bf16[2,5,512,512]{3,2,1,0:T(8,128)(2,1)} custom-call(bf16[2,5,512,512]{3,2,1,0:T(8,128)(2,1)} %band.1, s32[2,5]{1,0:T(2,128)} %occupancy.1), custom_call_target="tpu_custom_call" | custom-call | tf_op jit(solution)/shard_map/step/pallas_call | solution.py:274
  73.4 5.2 %copy.4 = bf16[2,5,512,512]{3,2,1,0:T(8,128)(2,1)} copy(bf16[2,5,512,512]{3,2,1,0:T(8,128)(2,1)} %step.1) | data formatting | bytes 10485760

commit v2 on v0

v2 whole, which is shorter than its diff:
```python
import jax
import jax.numpy as jnp
from jax import lax
from jax.experimental import pallas as pl
from jax.experimental.pallas import tpu as pltpu
from jax.sharding import PartitionSpec as P

F32, BF16 = jnp.float32, jnp.bfloat16
MESH = pl.DeviceIdType.MESH
B = 512
H = B // 2
OWN = 2
SLOTS = 5
SPAN = 6
MIB = 2**20
FACTOR = 0.5 / (SLOTS * B)
CORNER = ((2, 2), (2, 3), (3, 3))
INSIDE = [(row, col) for row in (2, 3) for col in range(row - 2, row + 3)]
EARLY = [(2, 0), (2, 1), (2, 2), (2, 3), (2, 4), (3, 1), (3, 2)]
LATE = [(3, 3), (3, 4), (3, 5)]


def chain(step):
    rows, cols = lax.axis_size("row"), lax.axis_size("col")
    place = lax.axis_index("row") * cols + lax.axis_index("col")
    other = lax.rem(place + (step + rows * cols), rows * cols)
    return {"row": lax.div(other, cols), "col": lax.rem(other, cols)}


def at(ref, row, col, height=1, width=1):
    return ref.at[row * B : (row + height) * B, col * B : (col + width) * B]


def product(left, right):
    return jnp.dot(left, right, preferred_element_type=F32)


def over(first, last, body):
    def step(n, carry):
        body(n, pl.multiple_of(n * B, B))
        return carry

    lax.fori_loop(first, last, step, 0)


def ramps():
    row = lax.broadcasted_iota(jnp.int32, (H, H), 0)
    col = lax.broadcasted_iota(jnp.int32, (H, H), 1)
    return row, col


def pack(block, piece):
    row, col = ramps()
    first, second = block[:H, :H].astype(F32), block[H:, H:].astype(F32)
    piece[:H, :H] = jnp.where(row <= col, first, second).astype(BF16)
    diagonal = jnp.sum(jnp.where(row == col, second, 0.0), axis=0, keepdims=True)
    piece[H:, :H] = jnp.broadcast_to(diagonal, (16, H)).astype(BF16)
    piece[H:, H:] = jnp.zeros((16, H), BF16)
    piece[:H, H:] = block[:H, H:]


def unpack(piece, block):
    row, col = ramps()
    tile = piece[:H, :H].astype(F32)
    turned = tile.T
    diagonal = piece[H : H + 16, :H].astype(F32)[:1]
    block[:H, :H] = jnp.where(row <= col, tile, turned).astype(BF16)
    block[H:, H:] = jnp.where(row > col, tile, jnp.where(row < col, turned, diagonal)).astype(BF16)
    side = piece[:H, H:]
    block[:H, H:] = side
    block[H:, :H] = side.T


def kernel(
    band, occupancy, done, base, last_square, last_rows,
    x, s, total, partial, packed, low, high,
    load_sem, send_sem, recv_sem,
):
    after, before = chain(1), chain(-1)
    barrier = pltpu.get_barrier_semaphore()
    for neighbour in (after, before):
        pl.semaphore_signal(barrier, inc=1, device_id=neighbour, device_id_type=MESH)

    def keep(row, col):
        return occupancy[row - OWN, col - (row - OWN)].astype(F32)

    order = [(2, 3), (3, 3), (2, 2)]
    order += [pair for pair in INSIDE if pair not in order]
    loads = {}
    for n, (row, col) in enumerate(order):
        loads[row, col] = pltpu.make_async_copy(
            band.at[row - 2, col - (row - 2)], at(x, row, col), load_sem.at[n]
        )
        loads[row, col].start()

    def loaded(row, col):
        loads[row, col].wait()
        block = at(x, row, col)
        block[...] = (block[...].astype(F32) * keep(row, col)).astype(BF16)

    sources = [packed.at[0], at(x, 2, 3), packed.at[1]]
    landings = [[low.at[0], at(x, 0, 1), low.at[1]], [high.at[0], at(x, 4, 5), high.at[1]]]
    copies = {}

    def send(side, n):
        copies[side, n] = pltpu.make_async_remote_copy(
            src_ref=sources[n],
            dst_ref=landings[side][n],
            send_sem=send_sem.at[side, n],
            recv_sem=recv_sem.at[side, n],
            device_id=(after, before)[side],
            device_id_type=MESH,
        )
        copies[side, n].start()

    loaded(2, 3)
    pl.semaphore_wait(barrier, 2)
    send(0, 1)
    loaded(3, 3)
    pack(at(x, 3, 3), packed.at[1])
    send(0, 2)
    loaded(2, 2)
    pack(at(x, 2, 2), packed.at[0])
    send(0, 0)

    for pair in order[3:]:
        loaded(*pair)
    for row, col in ((2, 0), (2, 1), (3, 1), (2, 4), (3, 4), (3, 5)):
        at(x, col, row)[...] = at(x, row, col)[...].T

    def square(row, col, first, last):
        value = product(at(x, row, first, 1, last - first)[...], at(x, first, col, last - first, 1)[...])
        at(s, row - 2, col)[...] = (value * keep(row, col)).astype(BF16)

    square(2, 2, 0, 5)
    square(3, 3, 1, 6)
    square(2, 3, 1, 5)
    at(s, 1, 2)[...] = at(s, 0, 3)[...].T

    def local(n, c):
        total[:, pl.ds(c, B)] = product(at(s, 0, 2, 2, 2)[...], x[2 * B : 4 * B, pl.ds(c, B)])

    over(1, 5, local)
    at(total, 0, 0)[...] = product(at(s, 0, 2)[...], at(x, 2, 0)[...])
    at(total, 1, 5)[...] = product(at(s, 1, 3)[...], at(x, 3, 5)[...])
    partial[:, :B] = product(at(x, 2, 2, 2, 2)[...], at(x, 2, 4, 2, 1)[...])
    partial[B:, B:] = product(at(x, 3, 3)[...], at(x, 3, 5)[...])

    def finish(row, col, value):
        scale = keep(row, col) * FACTOR
        block = 1.5 * at(x, row, col)[...].astype(F32) - scale * value
        if (row, col) in LATE:
            base[:, (col - 3) * B : (col - 2) * B] = block
        else:
            done[row - 2, col - (row - 2)] = block.astype(BF16)

    for n in (1, 2, 0):
        copies[0, n].wait_send()
    for n in range(3):
        send(1, n)
    copies[0, 1].wait_recv()
    at(x, 1, 0)[...] = at(x, 0, 1)[...].T
    copies[0, 2].wait_recv()
    unpack(low.at[1], at(x, 1, 1))
    square(2, 1, 0, 4)
    square(3, 1, 1, 4)
    copies[0, 0].wait_recv()
    unpack(low.at[0], at(x, 0, 0))
    square(2, 0, 0, 3)
    finish(2, 0, at(total, 0, 0)[...] + product(at(s, 0, 0, 1, 2)[...], at(x, 0, 0, 2, 1)[...]))
    finish(2, 1, at(total, 0, 1)[...] + product(at(s, 0, 0, 1, 2)[...], at(x, 0, 1, 2, 1)[...]))
    at(total, 0, 2)[...] += product(at(s, 0, 0, 1, 2)[...], at(x, 0, 2, 2, 1)[...])
    at(total, 0, 3)[...] += product(at(s, 0, 1)[...], at(x, 1, 3)[...])
    finish(3, 1, at(total, 1, 1)[...] + product(at(s, 1, 1)[...], at(x, 1, 1)[...]))
    for col in (2, 3):
        at(total, 1, col)[...] += product(at(s, 1, 1)[...], at(x, 1, col)[...])

    copies[1, 0].wait_recv()
    unpack(high.at[0], at(x, 4, 4))
    value = partial[:, :B] + product(at(x, 2, 4, 2, 1)[...], at(x, 4, 4)[...])
    at(s, 0, 4)[...] = (value[:B] * keep(2, 4)).astype(BF16)
    partial[B:, :B] = value[B:]
    for col in (2, 3, 4):
        finish(2, col, at(total, 0, col)[...] + product(at(s, 0, 4)[...], at(x, 4, col)[...]))
    copies[1, 1].wait_recv()
    at(x, 5, 4)[...] = at(x, 4, 5)[...].T
    value = partial[B:, :B] + product(at(x, 3, 5)[...], at(x, 5, 4)[...])
    at(s, 1, 4)[...] = (value * keep(3, 4)).astype(BF16)
    for col in (2, 3, 4, 5):
        finish(3, col, at(total, 1, col)[...] + product(at(s, 1, 4)[...], at(x, 4, col)[...]))
    partial[B:, B:] += product(at(x, 3, 4)[...], at(x, 4, 5)[...])
    last_rows[:, : 2 * B] = at(x, 5, 3, 1, 2)[...]
    copies[1, 2].wait_recv()
    unpack(high.at[1], last_rows.at[:, 2 * B :])
    value = partial[B:, B:] + product(at(x, 3, 5)[...], last_rows[:, 2 * B :])
    last_square[...] = (value * keep(3, 5)).astype(BF16)
    for n in range(3):
        copies[1, n].wait_send()


def tail(occupancy, done, base, last_square, last_rows, out, late, store_sem):
    stores = []

    def store(source, row, col):
        place = (row - 2, col - (row - 2))
        copy = pltpu.make_async_copy(source, out.at[place], store_sem.at[place])
        copy.start()
        stores.append(copy)

    for row, col in EARLY:
        store(done.at[row - 2, col - (row - 2)], row, col)
    for n, (row, col) in enumerate(LATE):
        scale = occupancy[row - 2, col - (row - 2)].astype(F32) * FACTOR
        value = product(last_square[...], last_rows[:, n * B : (n + 1) * B])
        late[n] = (base[:, n * B : (n + 1) * B] - scale * value).astype(BF16)
        store(late.at[n], row, col)
    for copy in stores:
        copy.wait()


def on_device(band_blocks, occupancy):
    dma = pltpu.SemaphoreType.DMA
    vmem = pl.BlockSpec(memory_space=pltpu.VMEM)
    smem = pl.BlockSpec(memory_space=pltpu.SMEM)
    hbm = pl.BlockSpec(memory_space=pl.ANY)
    held = pl.pallas_call(
        kernel,
        out_shape=(
            pltpu.VMEM(band_blocks.shape, BF16),
            pltpu.VMEM((B, 3 * B), F32),
            pltpu.VMEM((B, B), BF16),
            pltpu.VMEM((B, 3 * B), BF16),
        ),
        in_specs=[hbm, smem],
        out_specs=(vmem,) * 4,
        scratch_shapes=[
            pltpu.VMEM((SPAN * B, SPAN * B), BF16),
            pltpu.VMEM((OWN * B, SPAN * B), BF16),
            pltpu.VMEM((OWN * B, SPAN * B), F32),
            pltpu.VMEM((OWN * B, 2 * B), F32),
            pltpu.VMEM((2, H + 16, B), BF16),
            pltpu.VMEM((2, H + 16, B), BF16),
            pltpu.VMEM((2, H + 16, B), BF16),
            dma((OWN * SLOTS,)),
            dma((2, 3)),
            dma((2, 3)),
        ],
        compiler_params=pltpu.CompilerParams(
            collective_id=0, has_side_effects=True, vmem_limit_bytes=48 * MIB
        ),
        name="step",
    )(band_blocks, occupancy)
    return pl.pallas_call(
        tail,
        out_shape=jax.ShapeDtypeStruct(band_blocks.shape, BF16),
        in_specs=[smem] + [vmem] * 4,
        out_specs=hbm,
        scratch_shapes=[pltpu.VMEM((3, B, B), BF16), dma((OWN, SLOTS))],
        compiler_params=pltpu.CompilerParams(vmem_limit_bytes=12 * MIB),
        name="finish",
    )(occupancy, *held)


def solution(mesh):
    return jax.shard_map(
        on_device,
        mesh=mesh,
        in_specs=(P(("row", "col"), None, None, None), P(("row", "col"), None)),
        out_specs=P(("row", "col"), None, None, None),
        check_vma=False,
    )
```

time: 339 us -> 58.7 us (0.17)
  waiting for transfers between devices: 226 us -> 0 us
  matrix products: 71.7 us -> 0 us
  Pallas kernels: 0 us -> 57.7 us
  other arithmetic: 20 us -> 0 us
  local copies, waits for them, and re-layouts: 12.5 us -> 0.01 us
  starting transfers between devices: 8.21 us -> 0 us
    ppermute x2 -> x0, waiting for transfers between devices: 226 us -> none  [the longest x1 226 us: extended_2(): lax.ppermute(lax.slice_in_dim(block, block.shape[dim] - width, None, axis...]
    dot_general x10 -> x0, matrix products: 71.7 us -> none  [banded_product(): jnp.einsum('iqc,iscb->isqb', left_band[:, left_slot], neighbours, preferr...]
    pallas_call x0 -> x2, Pallas kernels: none -> 57.7 us  [the longest x1 54.7 us: on_device(): pl.pallas_call(kernel, out_shape=(pltpu.VMEM(band_blocks.shape, BF16), pl...]
    convert_element_type x3 -> x0, other arithmetic: 14.8 us -> none  [the longest x1 10.1 us: on_device(): (1.5 * masked.astype(jnp.float32) - factor * cubic).astype(jnp.bfloat16)]
    ppermute x2 -> x0, starting transfers between devices: 8.21 us -> none  [the longest x1 5.1 us: extended_2(): lax.ppermute(lax.slice_in_dim(block, 0, width, axis=dim), axis, backward)]
    scatter-add x2 -> x0, local copies, waits for them, and re-layouts: 7.07 us -> none  [banded_product(): running = running.at[:, first_out:last_out + 1].add(contribution)]
    convert_element_type x3 -> x0, local copies, waits for them, and re-layouts: 5.38 us -> none  [the longest x1 5.18 us: on_device(): (1.5 * masked.astype(jnp.float32) - factor * cubic).astype(jnp.bfloat16)]
    mul x1 -> x0, other arithmetic: 5.25 us -> none  [on_device(): masked = band_blocks * occupancy.astype(jnp.bfloat16)[:, :, None, None]]
  transfers between devices with their start and end apart: 2 -> 0, of which waited for: 1 -> 0; matrix products, arithmetic and copies ran while one was open for 8% -> 0% of each run, Pallas kernels for 0% -> 0%
where the time goes in v2:
time: 58.7 us; the launch traced here: 57.9 us
  Pallas kernels  57.7 us (98%)
    pallas_call x1, Pallas kernels, on_device(): pl.pallas_call(kernel, out_shape=(pltpu.VMEM(band_blocks.shape, BF16), pl...  54.7 us
    pallas_call x1, Pallas kernels, on_device(): pl.pallas_call(tail, out_shape=jax.ShapeDtypeStruct(band_blocks.shape, BF...  2.98 us

profile of v2, /device:TPU:0, one launch (start us, length us, event | category | flops | bytes accessed | tf_op | source)
XLA Modules:
  0.0 57.9 jit_solution(2890050969697568789)
XLA Ops:
  0.0 0.0 copy-start
  0.0 54.7 %step.1 = (bf16[2,5,512,512]{3,2,1,0:T(8,128)(2,1)S(1)}, f32[512,1536]{1,0:T(8,128)S(1)}, bf16[512,512]{1,0:T(8,128)(2,1)S(1)}, bf16[512,1536]{1,0:T(8,128)(2,1)S(1)}) custom-call(bf16[2,5,512,512]{3,2,1,0:T(8,128)(2,1)} %band.1, s32[2,5]{1,0:T(2,128)} %occupancy.3), custom_call_target="tpu_custom_call" | custom-call | tf_op jit(solution)/shard_map/step/pallas_call | solution.py:226
  54.7 0.0 copy-done
  54.7 3.0 %finish.1 = bf16[2,5,512,512]{3,2,1,0:T(8,128)(2,1)} custom-call(s32[2,5]{1,0:T(2,128)S(1)} %copy-done, bf16[2,5,512,512]{3,2,1,0:T(8,128)(2,1)S(1)} %get-tuple-element.9.done, f32[512,1536]{1,0:T(8,128)S(1)} %get-tuple-element.10.base, bf16[512,512]{1,0:T(8,128)(2,1)S(1)} %get-tuple-element.11.last_square, bf16[512,1536]{1,0:T(8,128)(2,1)S(1)} %get-tuple-element.12.last_rows), custom_call_target="tpu_custom_call" | custom-call | tf_op jit(solution)/shard_map/finish/pallas_call | solution.py:253
Async XLA Ops:
  0.0 54.7 %copy-start = (s32[2,5]{1,0:T(2,128)S(1)}, s32[2,5]{1,0:T(2,128)}, u32[]{:S(2)}) copy-start(s32[2,5]{1,0:T(2,128)} %occupancy.3) | copy-start | bytes 124

commit v3 on v2

v3 whole, which is shorter than its diff:
```python
import jax
import jax.numpy as jnp
from jax import lax
from jax.experimental import pallas as pl
from jax.experimental.pallas import tpu as pltpu
from jax.sharding import PartitionSpec as P

F32, BF16 = jnp.float32, jnp.bfloat16
MESH = pl.DeviceIdType.MESH
B = 512
H = B // 2
OWN = 2
SLOTS = 5
SPAN = 6
MIB = 2**20
FACTOR = 0.5 / (SLOTS * B)
CORNER = ((2, 2), (2, 3), (3, 3))
INSIDE = [(row, col) for row in (2, 3) for col in range(row - 2, row + 3)]
EARLY = [(2, 0), (2, 1), (2, 2), (2, 3), (2, 4), (3, 1), (3, 2)]
LATE = [(3, 3), (3, 4), (3, 5)]


def chain(step):
    rows, cols = lax.axis_size("row"), lax.axis_size("col")
    place = lax.axis_index("row") * cols + lax.axis_index("col")
    other = lax.rem(place + (step + rows * cols), rows * cols)
    return {"row": lax.div(other, cols), "col": lax.rem(other, cols)}


def at(ref, row, col, height=1, width=1):
    return ref.at[row * B : (row + height) * B, col * B : (col + width) * B]


def product(left, right):
    return jnp.dot(left, right, preferred_element_type=F32)


def over(first, last, body):
    def step(n, carry):
        body(n, pl.multiple_of(n * B, B))
        return carry

    lax.fori_loop(first, last, step, 0)


def ramps():
    row = lax.broadcasted_iota(jnp.int32, (H, H), 0)
    col = lax.broadcasted_iota(jnp.int32, (H, H), 1)
    return row, col


def pack(block, tile):
    row, col = ramps()
    first, second = block[:H, :H].astype(F32), block[H:, H:].astype(F32)
    tile[...] = jnp.where(row <= col, first, second).astype(BF16)
    diagonal = jnp.sum(jnp.where(row == col, second, 0.0), axis=0, keepdims=True)
    return [diagonal[:, : H // 2], diagonal[:, H // 2 :]]


def unpack_side(side, block):
    block[:H, H:] = side[...]
    block[H:, :H] = side[...].T


def unpack(tile, diagonals, n, block):
    row, col = ramps()
    tile = tile[...].astype(F32)
    turned = tile.T
    lines = diagonals[...].astype(F32)
    diagonal = jnp.concatenate([lines[2 * n : 2 * n + 1], lines[2 * n + 1 : 2 * n + 2]], axis=1)
    block[:H, :H] = jnp.where(row <= col, tile, turned).astype(BF16)
    block[H:, H:] = jnp.where(row > col, tile, jnp.where(row < col, turned, diagonal)).astype(BF16)


def kernel(
    band, occupied, done, base, part_square, left, last_rows, last_side, last_tile, last_diagonals,
    x, s, total, partial, packed, diagonals, low, low_diagonals, high,
    occupancy, load_sem, send_sem, recv_sem, ready,
):
    after, before = chain(1), chain(-1)
    barrier = pltpu.get_barrier_semaphore()
    pl.semaphore_signal(barrier, inc=1, device_id=before, device_id_type=MESH)

    def keep(row, col):
        return occupancy[row - OWN, col - (row - OWN)].astype(F32)

    order = [(2, 3), (3, 3), (2, 2)]
    order += [pair for pair in INSIDE if pair not in order]
    loads = {}
    for n, (row, col) in enumerate(order):
        loads[row, col] = pltpu.make_async_copy(
            band.at[row - 2, col - (row - 2)], at(x, row, col), load_sem.at[n]
        )
        loads[row, col].start()

    flags = pltpu.make_async_copy(occupied, occupancy, load_sem.at[len(order)])
    flags.start()

    def loaded(row, col):
        loads[row, col].wait()
        block = at(x, row, col)
        block[...] = (block[...].astype(F32) * keep(row, col)).astype(BF16)

    sources = [packed.at[0], packed.at[1], at(x, 2, 3), diagonals, band.at[0, 2, :H, H:], band.at[1, 2, :H, H:]]
    landings = [
        [low.at[0], low.at[1], at(x, 0, 1), low_diagonals, low.at[2], low.at[3]],
        [high.at[0], last_tile, at(x, 4, 5), last_diagonals, high.at[1], last_side],
    ]
    copies = {}

    for side in range(2):
        for n in range(6):
            copies[side, n] = pltpu.make_async_remote_copy(
                src_ref=sources[n],
                dst_ref=landings[side][n],
                send_sem=send_sem.at[side, n],
                recv_sem=recv_sem.at[side, n],
                device_id=(after, before)[side],
                device_id_type=MESH,
            )

    def send(side, n):
        copies[side, n].start()

    pl.semaphore_wait(barrier, 1)
    for n in (5, 4):
        send(0, n)
    pl.semaphore_signal(ready, inc=1, device_id=after, device_id_type=MESH)
    flags.wait()
    loaded(2, 3)
    send(0, 2)
    loaded(3, 3)
    second = pack(at(x, 3, 3), packed.at[1])
    loaded(2, 2)
    first = pack(at(x, 2, 2), packed.at[0])
    diagonals[...] = jnp.concatenate(first + second + [jnp.zeros((12, H // 2), F32)], axis=0).astype(BF16)
    for n in (3, 1, 0):
        send(0, n)

    for pair in order[3:]:
        loaded(*pair)
    for row, col in ((2, 0), (2, 1), (3, 1), (2, 4), (3, 4), (3, 5)):
        at(x, col, row)[...] = at(x, row, col)[...].T

    last_in_run = lax.axis_index("col") == lax.axis_size("col") - 1

    def send_before():
        for n in (4, 3, 0, 2, 5, 1):
            send(1, n)

    def square(row, col, first, last):
        value = product(at(x, row, first, 1, last - first)[...], at(x, first, col, last - first, 1)[...])
        at(s, row - 2, col)[...] = (value * keep(row, col)).astype(BF16)

    square(2, 2, 0, 5)
    square(3, 3, 1, 6)
    pl.semaphore_wait(ready, 1)

    @pl.when(jnp.logical_not(last_in_run))
    def _():
        send_before()

    square(2, 3, 1, 5)
    at(s, 1, 2)[...] = at(s, 0, 3)[...].T

    def local(n, c):
        total[:, pl.ds(c, B)] = product(at(s, 0, 2, 2, 2)[...], x[2 * B : 4 * B, pl.ds(c, B)])

    over(1, 5, local)
    at(total, 0, 0)[...] = product(at(s, 0, 2)[...], at(x, 2, 0)[...])
    at(total, 1, 5)[...] = product(at(s, 1, 3)[...], at(x, 3, 5)[...])
    partial[:, :B] = product(at(x, 2, 2, 2, 2)[...], at(x, 2, 4, 2, 1)[...])
    partial[B:, B:] = product(at(x, 3, 3)[...], at(x, 3, 5)[...])

    def finish(row, col, value):
        scale = keep(row, col) * FACTOR
        block = 1.5 * at(x, row, col)[...].astype(F32) - scale * value
        if (row, col) in LATE:
            base[:, (col - 3) * B : (col - 2) * B] = block
        else:
            done[row - 2, col - (row - 2)] = block.astype(BF16)

    @pl.when(last_in_run)
    def _():
        for n in range(6):
            copies[0, n].wait_send()
        send_before()

    def near_corner():
        copies[1, 4].wait_recv()
        unpack_side(high.at[1], at(x, 4, 4))
        copies[1, 3].wait_recv()
        copies[1, 0].wait_recv()
        unpack(high.at[0], last_diagonals, 0, at(x, 4, 4))
        value = partial[:, :B] + product(at(x, 2, 4, 2, 1)[...], at(x, 4, 4)[...])
        at(s, 0, 4)[...] = (value[:B] * keep(2, 4)).astype(BF16)
        partial[B:, :B] = value[B:]
        for col in (2, 3):
            at(total, 0, col)[...] += product(at(s, 0, 4)[...], at(x, 4, col)[...])
        finish(2, 4, at(total, 0, 4)[...] + product(at(s, 0, 4)[...], at(x, 4, 4)[...]))

    first_in_run = lax.axis_index("col") == 0
    pl.when(first_in_run)(near_corner)

    copies[0, 5].wait_recv()
    unpack_side(low.at[3], at(x, 1, 1))
    copies[0, 4].wait_recv()
    unpack_side(low.at[2], at(x, 0, 0))
    copies[0, 2].wait_recv()
    at(x, 1, 0)[...] = at(x, 0, 1)[...].T
    copies[0, 3].wait_recv()
    copies[0, 1].wait_recv()
    unpack(low.at[1], low_diagonals, 1, at(x, 1, 1))
    square(2, 1, 0, 4)
    square(3, 1, 1, 4)
    copies[0, 0].wait_recv()
    unpack(low.at[0], low_diagonals, 0, at(x, 0, 0))
    square(2, 0, 0, 3)
    finish(2, 0, at(total, 0, 0)[...] + product(at(s, 0, 0, 1, 2)[...], at(x, 0, 0, 2, 1)[...]))
    finish(2, 1, at(total, 0, 1)[...] + product(at(s, 0, 0, 1, 2)[...], at(x, 0, 1, 2, 1)[...]))
    at(total, 0, 2)[...] += product(at(s, 0, 0, 1, 2)[...], at(x, 0, 2, 2, 1)[...])
    at(total, 0, 3)[...] += product(at(s, 0, 1)[...], at(x, 1, 3)[...])
    finish(3, 1, at(total, 1, 1)[...] + product(at(s, 1, 1)[...], at(x, 1, 1)[...]))
    for col in (2, 3):
        at(total, 1, col)[...] += product(at(s, 1, 1)[...], at(x, 1, col)[...])

    pl.when(jnp.logical_not(first_in_run))(near_corner)
    for col in (2, 3):
        finish(2, col, at(total, 0, col)[...])

    copies[1, 2].wait_recv()
    at(x, 5, 4)[...] = at(x, 4, 5)[...].T
    value = partial[B:, :B] + product(at(x, 3, 5)[...], at(x, 5, 4)[...])
    at(s, 1, 4)[...] = (value * keep(3, 4)).astype(BF16)
    for col in (2, 3, 4, 5):
        finish(3, col, at(total, 1, col)[...] + product(at(s, 1, 4)[...], at(x, 4, col)[...]))
    value = partial[B:, B:] + product(at(x, 3, 4)[...], at(x, 4, 5)[...])
    last_rows[...] = at(x, 5, 3, 1, 2)[...]
    left[...] = at(x, 3, 5)[...]
    copies[1, 5].wait_recv()
    part_square[:, :H] = value[:, :H] + product(left[:, H:], last_side[...].T)
    part_square[:, H:] = value[:, H:] + product(left[:, :H], last_side[...])
    copies[1, 1].wait_recv()
    for n in range(6):
        copies[1, n].wait_send()

    @pl.when(jnp.logical_not(last_in_run))
    def _():
        for n in range(6):
            copies[0, n].wait_send()


def tail(occupancy, done, base, part_square, left, last_rows, last_side, last_tile, last_diagonals, out, corner, late, store_sem):
    stores = []

    def store(source, row, col):
        place = (row - 2, col - (row - 2))
        copy = pltpu.make_async_copy(source, out.at[place], store_sem.at[place])
        copy.start()
        stores.append(copy)

    for row, col in EARLY:
        store(done.at[row - 2, col - (row - 2)], row, col)
    unpack_side(last_side, corner)
    unpack(last_tile, last_diagonals, 1, corner)
    squares = []
    for half in (slice(0, H), slice(H, B)):
        value = part_square[:, half] + product(left[:, half], corner[half, half])
        squares.append((value * occupancy[1, 4].astype(F32)).astype(BF16))
    square = jnp.concatenate(squares, axis=1)
    rows = [last_rows.at[:, :B], last_rows.at[:, B:], corner]
    for n, (row, col) in enumerate(LATE):
        scale = occupancy[row - 2, col - (row - 2)].astype(F32) * FACTOR
        value = product(square, rows[n][...])
        late[n] = (base[:, n * B : (n + 1) * B] - scale * value).astype(BF16)
        store(late.at[n], row, col)
    for copy in stores:
        copy.wait()


def on_device(band_blocks, occupancy):
    dma = pltpu.SemaphoreType.DMA
    vmem = pl.BlockSpec(memory_space=pltpu.VMEM)
    smem = pl.BlockSpec(memory_space=pltpu.SMEM)
    hbm = pl.BlockSpec(memory_space=pl.ANY)
    held = pl.pallas_call(
        kernel,
        out_shape=(
            pltpu.VMEM(band_blocks.shape, BF16),
            pltpu.VMEM((B, 3 * B), F32),
            pltpu.VMEM((B, B), F32),
            pltpu.VMEM((B, B), BF16),
            pltpu.VMEM((B, 2 * B), BF16),
            pltpu.VMEM((H, H), BF16),
            pltpu.VMEM((H, H), BF16),
            pltpu.VMEM((16, H // 2), BF16),
        ),
        in_specs=[hbm, hbm],
        out_specs=(vmem,) * 8,
        scratch_shapes=[
            pltpu.VMEM((SPAN * B, SPAN * B), BF16),
            pltpu.VMEM((OWN * B, SPAN * B), BF16),
            pltpu.VMEM((OWN * B, SPAN * B), F32),
            pltpu.VMEM((OWN * B, 2 * B), F32),
            pltpu.VMEM((2, H, H), BF16),
            pltpu.VMEM((16, H // 2), BF16),
            pltpu.VMEM((4, H, H), BF16),
            pltpu.VMEM((16, H // 2), BF16),
            pltpu.VMEM((2, H, H), BF16),
            pltpu.SMEM((OWN, SLOTS), jnp.int32),
            dma((OWN * SLOTS + 1,)),
            dma((2, 6)),
            dma((2, 6)),
            pltpu.SemaphoreType.REGULAR,
        ],
        compiler_params=pltpu.CompilerParams(
            collective_id=0, has_side_effects=True, vmem_limit_bytes=48 * MIB
        ),
        name="step",
    )(band_blocks, occupancy)
    return pl.pallas_call(
        tail,
        out_shape=jax.ShapeDtypeStruct(band_blocks.shape, BF16),
        in_specs=[smem] + [vmem] * 8,
        out_specs=hbm,
        scratch_shapes=[pltpu.VMEM((B, B), BF16), pltpu.VMEM((3, B, B), BF16), dma((OWN, SLOTS))],
        compiler_params=pltpu.CompilerParams(vmem_limit_bytes=12 * MIB),
        name="finish",
    )(occupancy, *held)


def solution(mesh):
    return jax.shard_map(
        on_device,
        mesh=mesh,
        in_specs=(P(("row", "col"), None, None, None), P(("row", "col"), None)),
        out_specs=P(("row", "col"), None, None, None),
        check_vma=False,
    )
```

time: 58.7 us -> 54.4 us (0.927); the launches traced: 57.9 us -> 54.3 us
  Pallas kernels: 57.7 us -> 54.1 us
    pallas_call x1, Pallas kernels: 54.7 us -> 51.1 us  [on_device(): pl.pallas_call(kernel, out_shape=(pltpu.VMEM(band_blocks.shape, BF16), pl...]
where the time goes in v3:
time: 54.4 us; the launch traced here: 54.3 us
  Pallas kernels  54.1 us (99%)
    pallas_call x1, Pallas kernels, on_device(): pl.pallas_call(kernel, out_shape=(pltpu.VMEM(band_blocks.shape, BF16), pl...  51.1 us
    pallas_call x1, Pallas kernels, on_device(): pl.pallas_call(tail, out_shape=jax.ShapeDtypeStruct(band_blocks.shape, BF...  2.97 us

profile of v3, /device:TPU:0, one launch (start us, length us, event | category | flops | bytes accessed | tf_op | source)
XLA Modules:
  0.0 54.3 jit_solution(17720131348559034613)
XLA Ops:
  0.0 0.0 copy-start
  0.0 51.1 %step.1 = (bf16[2,5,512,512]{3,2,1,0:T(8,128)(2,1)S(1)}, f32[512,1536]{1,0:T(8,128)S(1)}, f32[512,512]{1,0:T(8,128)S(1)}, bf16[512,512]{1,0:T(8,128)(2,1)S(1)}, ...) custom-call(bf16[2,5,512,512]{3,2,1,0:T(8,128)(2,1)} %band.1, ...), custom_call_target="tpu_custom_call" | custom-call | tf_op jit(solution)/shard_map/step/pallas_call | solution.py:286
  51.1 0.0 copy-done
  51.1 3.0 %finish.1 = bf16[2,5,512,512]{3,2,1,0:T(8,128)(2,1)} custom-call(s32[2,5]{1,0:T(2,128)S(1)} %copy-done, bf16[2,5,512,512]{3,2,1,0:T(8,128)(2,1)S(1)} %get-tuple-element.13.done, f32[512,1536]{1,0:T(8,128)S(1)} %get-tuple-element.14.base, f32[512,512]{1,0:T(8,128)S(1)} %get-tuple-element.15.part_square, bf16[512,512]{1,0:T(8,128)(2,1)S(1)} %get-tuple-element.16.left, ...), custom_call_target="tpu_custom_call" | custom-call | tf_op jit(solution)/shard_map/finish/pallas_call | solution.py:321
Async XLA Ops:
  0.0 51.1 %copy-start = (s32[2,5]{1,0:T(2,128)S(1)}, s32[2,5]{1,0:T(2,128)}, u32[]{:S(2)}) copy-start(s32[2,5]{1,0:T(2,128)} %occupancy.1) | copy-start | bytes 124

commit v4 on v3

--- a/solution.py
+++ b/solution.py
@@ -78,8 +78,23 @@
     occupancy, load_sem, send_sem, recv_sem, ready,
 ):
     after, before = chain(1), chain(-1)
+    place, last = lax.axis_index("col"), lax.axis_size("col") - 1
+    first_in_run, last_in_run = place == 0, place == last
+    inside_run = jnp.logical_not(jnp.logical_or(first_in_run, last_in_run))
+
+    def signal(semaphore, device):
+        pl.semaphore_signal(semaphore, inc=1, device_id=device, device_id_type=MESH)
+
     barrier = pltpu.get_barrier_semaphore()
-    pl.semaphore_signal(barrier, inc=1, device_id=before, device_id_type=MESH)
+
+    @pl.when(jnp.logical_not(last_in_run))
+    def _():
+        signal(barrier, after)
+
+    @pl.when(place <= 1)
+    def _():
+        signal(barrier, before)
+
 
     def keep(row, col):
         return occupancy[row - OWN, col - (row - OWN)].astype(F32)
@@ -122,10 +137,33 @@
     def send(side, n):
         copies[side, n].start()
 
-    pl.semaphore_wait(barrier, 1)
+
+    @pl.when(last_in_run)
+    def _():
+        pl.semaphore_wait(barrier, 2)
+
+    @pl.when(jnp.logical_not(last_in_run))
+    def _():
+        pl.semaphore_wait(barrier, 1)
+
+    @pl.when(inside_run)
+    def _():
+        send(1, 4)
+
+    @pl.when(place >= 2)
+    def _():
+        signal(ready, before)
+
+    @pl.when(last_in_run)
+    def _():
+        signal(ready, after)
+
+    @pl.when(inside_run)
+    def _():
+        pl.semaphore_wait(ready, 1)
+
     for n in (5, 4):
         send(0, n)
-    pl.semaphore_signal(ready, inc=1, device_id=after, device_id_type=MESH)
     flags.wait()
     loaded(2, 3)
     send(0, 2)
@@ -142,10 +180,8 @@
     for row, col in ((2, 0), (2, 1), (3, 1), (2, 4), (3, 4), (3, 5)):
         at(x, col, row)[...] = at(x, row, col)[...].T
 
-    last_in_run = lax.axis_index("col") == lax.axis_size("col") - 1
-
     def send_before():
-        for n in (4, 3, 0, 2, 5, 1):
+        for n in (3, 0, 2, 5, 1):
             send(1, n)
 
     def square(row, col, first, last):
@@ -154,7 +190,11 @@
 
     square(2, 2, 0, 5)
     square(3, 3, 1, 6)
-    pl.semaphore_wait(ready, 1)
+
+    @pl.when(first_in_run)
+    def _():
+        pl.semaphore_wait(ready, 1)
+        send(1, 4)
 
     @pl.when(jnp.logical_not(last_in_run))
     def _():
@@ -171,6 +211,11 @@
     at(total, 1, 5)[...] = product(at(s, 1, 3)[...], at(x, 3, 5)[...])
     partial[:, :B] = product(at(x, 2, 2, 2, 2)[...], at(x, 2, 4, 2, 1)[...])
     partial[B:, B:] = product(at(x, 3, 3)[...], at(x, 3, 5)[...])
+    part20, part21, part31 = partial.at[:B, B:], at(total, 0, 5), at(total, 1, 0)
+    part20[...] = product(at(x, 2, 2)[...], at(x, 2, 0)[...])
+    value = product(at(x, 2, 2, 2, 2)[...], at(x, 2, 1, 2, 1)[...])
+    part21[...] = value[:B]
+    part31[...] = value[B:]
 
     def finish(row, col, value):
         scale = keep(row, col) * FACTOR
@@ -184,6 +229,7 @@
     def _():
         for n in range(6):
             copies[0, n].wait_send()
+        send(1, 4)
         send_before()
 
     def near_corner():
@@ -199,7 +245,6 @@
             at(total, 0, col)[...] += product(at(s, 0, 4)[...], at(x, 4, col)[...])
         finish(2, 4, at(total, 0, 4)[...] + product(at(s, 0, 4)[...], at(x, 4, 4)[...]))
 
-    first_in_run = lax.axis_index("col") == 0
     pl.when(first_in_run)(near_corner)
 
     copies[0, 5].wait_recv()
@@ -208,21 +253,23 @@
     unpack_side(low.at[2], at(x, 0, 0))
     copies[0, 2].wait_recv()
     at(x, 1, 0)[...] = at(x, 0, 1)[...].T
+    part20[...] += product(at(x, 2, 1)[...], at(x, 1, 0)[...])
+    part21[...] += product(at(x, 2, 0)[...], at(x, 0, 1)[...])
     copies[0, 3].wait_recv()
     copies[0, 1].wait_recv()
     unpack(low.at[1], low_diagonals, 1, at(x, 1, 1))
-    square(2, 1, 0, 4)
-    square(3, 1, 1, 4)
-    copies[0, 0].wait_recv()
-    unpack(low.at[0], low_diagonals, 0, at(x, 0, 0))
-    square(2, 0, 0, 3)
-    finish(2, 0, at(total, 0, 0)[...] + product(at(s, 0, 0, 1, 2)[...], at(x, 0, 0, 2, 1)[...]))
-    finish(2, 1, at(total, 0, 1)[...] + product(at(s, 0, 0, 1, 2)[...], at(x, 0, 1, 2, 1)[...]))
-    at(total, 0, 2)[...] += product(at(s, 0, 0, 1, 2)[...], at(x, 0, 2, 2, 1)[...])
+    at(s, 0, 1)[...] = ((part21[...] + product(at(x, 2, 1)[...], at(x, 1, 1)[...])) * keep(2, 1)).astype(BF16)
+    at(s, 1, 1)[...] = ((part31[...] + product(at(x, 3, 1)[...], at(x, 1, 1)[...])) * keep(3, 1)).astype(BF16)
     at(total, 0, 3)[...] += product(at(s, 0, 1)[...], at(x, 1, 3)[...])
     finish(3, 1, at(total, 1, 1)[...] + product(at(s, 1, 1)[...], at(x, 1, 1)[...]))
     for col in (2, 3):
         at(total, 1, col)[...] += product(at(s, 1, 1)[...], at(x, 1, col)[...])
+    copies[0, 0].wait_recv()
+    unpack(low.at[0], low_diagonals, 0, at(x, 0, 0))
+    at(s, 0, 0)[...] = ((part20[...] + product(at(x, 2, 0)[...], at(x, 0, 0)[...])) * keep(2, 0)).astype(BF16)
+    finish(2, 0, at(total, 0, 0)[...] + product(at(s, 0, 0, 1, 2)[...], at(x, 0, 0, 2, 1)[...]))
+    finish(2, 1, at(total, 0, 1)[...] + product(at(s, 0, 0, 1, 2)[...], at(x, 0, 1, 2, 1)[...]))
+    at(total, 0, 2)[...] += product(at(s, 0, 0, 1, 2)[...], at(x, 0, 2, 2, 1)[...])
 
     pl.when(jnp.logical_not(first_in_run))(near_corner)
     for col in (2, 3):

time: 54.4 us -> 53.8 us (0.989)
  Pallas kernels: 54.1 us -> 53.5 us
    pallas_call x1, Pallas kernels: 51.1 us -> 50.5 us  [on_device(): pl.pallas_call(kernel, out_shape=(pltpu.VMEM(band_blocks.shape, BF16), pl...]
where the time goes in v4:
time: 53.8 us; the launch traced here: 53.7 us
  Pallas kernels  53.5 us (99%)
    pallas_call x1, Pallas kernels, on_device(): pl.pallas_call(kernel, out_shape=(pltpu.VMEM(band_blocks.shape, BF16), pl...  50.5 us
    pallas_call x1, Pallas kernels, on_device(): pl.pallas_call(tail, out_shape=jax.ShapeDtypeStruct(band_blocks.shape, BF...  2.97 us

profile of v4, /device:TPU:0, one launch (start us, length us, event | category | flops | bytes accessed | tf_op | source)
XLA Modules:
  0.0 53.7 jit_solution(7624050666316016244)
XLA Ops:
  0.0 0.0 copy-start
  0.0 50.5 %step.1 = (bf16[2,5,512,512]{3,2,1,0:T(8,128)(2,1)S(1)}, f32[512,1536]{1,0:T(8,128)S(1)}, f32[512,512]{1,0:T(8,128)S(1)}, bf16[512,512]{1,0:T(8,128)(2,1)S(1)}, ...) custom-call(bf16[2,5,512,512]{3,2,1,0:T(8,128)(2,1)} %band.1, ...), custom_call_target="tpu_custom_call" | custom-call | tf_op jit(solution)/shard_map/step/pallas_call | solution.py:333
  50.5 0.0 copy-done
  50.5 3.0 %finish.1 = bf16[2,5,512,512]{3,2,1,0:T(8,128)(2,1)} custom-call(s32[2,5]{1,0:T(2,128)S(1)} %copy-done, bf16[2,5,512,512]{3,2,1,0:T(8,128)(2,1)S(1)} %get-tuple-element.13.done, f32[512,1536]{1,0:T(8,128)S(1)} %get-tuple-element.14.base, f32[512,512]{1,0:T(8,128)S(1)} %get-tuple-element.15.part_square, bf16[512,512]{1,0:T(8,128)(2,1)S(1)} %get-tuple-element.16.left, ...), custom_call_target="tpu_custom_call" | custom-call | tf_op jit(solution)/shard_map/finish/pallas_call | solution.py:368
Async XLA Ops:
  0.0 50.5 %copy-start = (s32[2,5]{1,0:T(2,128)S(1)}, s32[2,5]{1,0:T(2,128)}, u32[]{:S(2)}) copy-start(s32[2,5]{1,0:T(2,128)} %occupancy.1) | copy-start | bytes 124

commit v5 on v3

--- a/solution.py
+++ b/solution.py
@@ -15,6 +15,10 @@
 MIB = 2**20
 FACTOR = 0.5 / (SLOTS * B)
 CORNER = ((2, 2), (2, 3), (3, 3))
+PIECES = 9
+STRIPS = (2, 3, 4, 5)
+OTHERS = (0, 1, 6, 7, 8)
+STRIP = B // len(STRIPS)
 INSIDE = [(row, col) for row in (2, 3) for col in range(row - 2, row + 3)]
 EARLY = [(2, 0), (2, 1), (2, 2), (2, 3), (2, 4), (3, 1), (3, 2)]
 LATE = [(3, 3), (3, 4), (3, 5)]
@@ -74,17 +78,60 @@
 
 def kernel(
     band, occupied, done, base, part_square, left, last_rows, last_side, last_tile, last_diagonals,
-    x, s, total, partial, packed, diagonals, low, low_diagonals, high,
+    x, s, total, partial, packed, diagonals, tiles, sides, lines,
     occupancy, load_sem, send_sem, recv_sem, ready,
 ):
-    after, before = chain(1), chain(-1)
+    place, last = lax.axis_index("col"), lax.axis_size("col") - 1
+    parity = lax.rem(place, 2)
+    even, odd = parity == 0, parity == 1
+    first_in_run, last_in_run = place == 0, place == last
+    step = 1 - 2 * parity
+    partner, target, origin = chain(step), chain(2 * step), chain(-2 * step)
+    low, high = 1 - parity, parity
+    cols = last + 1
+    odd_run = lax.rem(lax.axis_index("row"), 2) == 1
+    even_run = jnp.logical_not(odd_run)
+    head, foot = place <= 1, place >= last - 1
+    far = jnp.logical_or(jnp.logical_and(odd_run, foot), jnp.logical_and(even_run, head))
+    relay = jnp.logical_and(jnp.logical_or(head, foot), jnp.logical_not(far))
+    ends = jnp.logical_or(first_in_run, last_in_run)
+    crossing = jnp.logical_and(far, ends)
+    spared = jnp.logical_and(far, jnp.logical_not(ends))
+    other_end = chain(jnp.where(head, last - 1, 1 - last))
+    beyond = chain(jnp.where(head, cols - place, last - place - cols))
+
+    def signal(semaphore, device):
+        pl.semaphore_signal(semaphore, inc=1, device_id=device, device_id_type=MESH)
+
+    def when(condition, *more):
+        for other in more:
+            condition = jnp.logical_and(condition, other)
+        return pl.when(condition)
+
     barrier = pltpu.get_barrier_semaphore()
-    pl.semaphore_signal(barrier, inc=1, device_id=before, device_id_type=MESH)
+    signal(barrier, partner)
+
+    @when(jnp.logical_not(last_in_run), jnp.logical_not(jnp.logical_and(first_in_run, even_run)))
+    def _():
+        signal(barrier, origin)
+
+    @when(head)
+    def _():
+        signal(barrier, other_end)
+
+    @when(place == 1, odd_run)
+    def _():
+        signal(barrier, chain(-2))
+
+    @when(crossing)
+    def _():
+        for n in (0, 1):
+            signal(barrier, chain(jnp.where(last_in_run, cols - n, n - cols)))
 
     def keep(row, col):
         return occupancy[row - OWN, col - (row - OWN)].astype(F32)
 
-    order = [(2, 3), (3, 3), (2, 2)]
+    order = [(2, 3), (2, 2), (3, 3)]
     order += [pair for pair in INSIDE if pair not in order]
     loads = {}
     for n, (row, col) in enumerate(order):
@@ -92,7 +139,6 @@
             band.at[row - 2, col - (row - 2)], at(x, row, col), load_sem.at[n]
         )
         loads[row, col].start()
-
     flags = pltpu.make_async_copy(occupied, occupancy, load_sem.at[len(order)])
     flags.start()
 
@@ -101,76 +147,138 @@
         block = at(x, row, col)
         block[...] = (block[...].astype(F32) * keep(row, col)).astype(BF16)
 
-    sources = [packed.at[0], packed.at[1], at(x, 2, 3), diagonals, band.at[0, 2, :H, H:], band.at[1, 2, :H, H:]]
-    landings = [
-        [low.at[0], low.at[1], at(x, 0, 1), low_diagonals, low.at[2], low.at[3]],
-        [high.at[0], last_tile, at(x, 4, 5), last_diagonals, high.at[1], last_side],
-    ]
-    copies = {}
-
-    for side in range(2):
-        for n in range(6):
-            copies[side, n] = pltpu.make_async_remote_copy(
-                src_ref=sources[n],
-                dst_ref=landings[side][n],
-                send_sem=send_sem.at[side, n],
-                recv_sem=recv_sem.at[side, n],
-                device_id=(after, before)[side],
-                device_id_type=MESH,
-            )
-
-    def send(side, n):
-        copies[side, n].start()
-
-    pl.semaphore_wait(barrier, 1)
-    for n in (5, 4):
-        send(0, n)
-    pl.semaphore_signal(ready, inc=1, device_id=after, device_id_type=MESH)
+    def landing(slot, n):
+        if n < 2:
+            return tiles.at[slot, n]
+        if n < 6:
+            return sides.at[slot, (n - 2) * STRIP : (n - 1) * STRIP]
+        return lines.at[slot] if n == 6 else tiles.at[slot, n - 5]
+
+    def strip(n):
+        return x.at[2 * B + (n - 2) * STRIP : 2 * B + (n - 1) * STRIP, 3 * B : 4 * B]
+
+    sources = [band.at[0, 2, :H, H:], band.at[1, 2, :H, H:]] + [strip(n) for n in STRIPS]
+    sources += [diagonals, packed.at[0], packed.at[1]]
+
+    def remote(source, slot, kind, n, device):
+        return pltpu.make_async_remote_copy(
+            src_ref=source,
+            dst_ref=landing(slot, n),
+            send_sem=send_sem.at[kind, n],
+            recv_sem=recv_sem.at[slot, n],
+            device_id=device,
+            device_id_type=MESH,
+        )
+
+    direct = [remote(sources[n], 0, 0, n, partner) for n in range(PIECES)]
+    onward = [remote(landing(0, n), 1, 1, n, target) for n in range(PIECES)]
+    aside = {n: remote(landing(0, n), 2, 1, n, other_end) for n in OTHERS}
+    across = {n: remote(strip(n), 2, 2, n, other_end) for n in STRIPS}
+    relays = [remote(landing(2, n), 1, 2, n, beyond) for n in range(PIECES)]
+
+    def forward(n):
+        direct[n].wait_recv()
+        when(jnp.logical_not(spared))(onward[n].start)
+        if n in OTHERS:
+            when(spared)(aside[n].start)
+
+    def pass_on(condition, pieces):
+        @when(relay, condition)
+        def _():
+            for n in pieces:
+                across[n].wait_recv() if n in STRIPS else aside[n].wait_recv()
+                relays[n].start()
+
+    def arrived(relayed, *pieces):
+        @when(relayed)
+        def _():
+            for n in pieces:
+                onward[n].wait_recv()
+
+    for run, counts in ((odd_run, (3, 2, 2, 3)), (even_run, (2, 1, 4, 5))):
+        for position, count in zip((0, 1, last - 1, last), counts):
+
+            @when(run, place == position)
+            def _():
+                pl.semaphore_wait(barrier, count)
+
+    @when(jnp.logical_not(jnp.logical_or(head, foot)))
+    def _():
+        pl.semaphore_wait(barrier, 2)
+
+    @when(even_run, foot)
+    def _():
+        signal(ready, other_end)
+
+    @when(even_run, last_in_run)
+    def _():
+        signal(ready, chain(2))
+
+    direct[0].start()
+    direct[1].start()
     flags.wait()
     loaded(2, 3)
-    send(0, 2)
+    for n in STRIPS:
+        direct[n].start()
+    loaded(2, 2)
+    first = pack(at(x, 2, 2), packed.at[0])
     loaded(3, 3)
     second = pack(at(x, 3, 3), packed.at[1])
-    loaded(2, 2)
-    first = pack(at(x, 2, 2), packed.at[0])
     diagonals[...] = jnp.concatenate(first + second + [jnp.zeros((12, H // 2), F32)], axis=0).astype(BF16)
-    for n in (3, 1, 0):
-        send(0, n)
+    for n in (6, 7, 8):
+        direct[n].start()
+
+    @when(crossing, last_in_run)
+    def _():
+        for n in STRIPS:
+            across[n].start()
 
     for pair in order[3:]:
         loaded(*pair)
     for row, col in ((2, 0), (2, 1), (3, 1), (2, 4), (3, 4), (3, 5)):
         at(x, col, row)[...] = at(x, row, col)[...].T
 
-    last_in_run = lax.axis_index("col") == lax.axis_size("col") - 1
-
-    def send_before():
-        for n in (4, 3, 0, 2, 5, 1):
-            send(1, n)
-
     def square(row, col, first, last):
         value = product(at(x, row, first, 1, last - first)[...], at(x, first, col, last - first, 1)[...])
         at(s, row - 2, col)[...] = (value * keep(row, col)).astype(BF16)
 
     square(2, 2, 0, 5)
+
+    @when(jnp.logical_or(place == 1, jnp.logical_and(first_in_run, even_run)))
+    def _():
+        pl.semaphore_wait(ready, 1)
+
+    @when(crossing, first_in_run)
+    def _():
+        for n in STRIPS:
+            across[n].start()
+
+    forward(0)
     square(3, 3, 1, 6)
-    pl.semaphore_wait(ready, 1)
-
-    @pl.when(jnp.logical_not(last_in_run))
-    def _():
-        send_before()
-
+    forward(1)
     square(2, 3, 1, 5)
     at(s, 1, 2)[...] = at(s, 0, 3)[...].T
 
     def local(n, c):
         total[:, pl.ds(c, B)] = product(at(s, 0, 2, 2, 2)[...], x[2 * B : 4 * B, pl.ds(c, B)])
 
-    over(1, 5, local)
+    over(1, 3, local)
+    forward(2)
+    over(3, 5, local)
     at(total, 0, 0)[...] = product(at(s, 0, 2)[...], at(x, 2, 0)[...])
+    forward(3)
     at(total, 1, 5)[...] = product(at(s, 1, 3)[...], at(x, 3, 5)[...])
     partial[:, :B] = product(at(x, 2, 2, 2, 2)[...], at(x, 2, 4, 2, 1)[...])
     partial[B:, B:] = product(at(x, 3, 3)[...], at(x, 3, 5)[...])
+    forward(4)
+    part20, part21, part31 = partial.at[:B, B:], at(total, 0, 5), at(total, 1, 0)
+    part20[...] = product(at(x, 2, 2)[...], at(x, 2, 0)[...])
+    value = product(at(x, 2, 2, 2, 2)[...], at(x, 2, 1, 2, 1)[...])
+    part21[...] = value[:B]
+    part31[...] = value[B:]
+    left[...] = at(x, 3, 5)[...]
+    last_rows[:, :B] = at(x, 5, 3)[...]
+    forward(5)
 
     def finish(row, col, value):
         scale = keep(row, col) * FACTOR
@@ -180,18 +288,37 @@
         else:
             done[row - 2, col - (row - 2)] = block.astype(BF16)
 
-    @pl.when(last_in_run)
-    def _():
-        for n in range(6):
-            copies[0, n].wait_send()
-        send_before()
-
-    def near_corner():
-        copies[1, 4].wait_recv()
-        unpack_side(high.at[1], at(x, 4, 4))
-        copies[1, 3].wait_recv()
-        copies[1, 0].wait_recv()
-        unpack(high.at[0], last_diagonals, 0, at(x, 4, 4))
+    def low_01():
+        arrived(even, *STRIPS)
+        at(x, 0, 1)[...] = sides[low]
+        at(x, 1, 0)[...] = sides[low].T
+        part20[...] += product(at(x, 2, 1)[...], at(x, 1, 0)[...])
+        part21[...] += product(at(x, 2, 0)[...], at(x, 0, 1)[...])
+
+    def low_00():
+        arrived(even, 0, 6, 7)
+        unpack_side(tiles.at[low, 0], at(x, 0, 0))
+        unpack(tiles.at[low, 2], lines.at[low], 0, at(x, 0, 0))
+        at(s, 0, 0)[...] = ((part20[...] + product(at(x, 2, 0)[...], at(x, 0, 0)[...])) * keep(2, 0)).astype(BF16)
+
+    def low_11():
+        arrived(even, 1, 8)
+        unpack_side(tiles.at[low, 1], at(x, 1, 1))
+        unpack(tiles.at[low, 3], lines.at[low], 1, at(x, 1, 1))
+        at(s, 0, 1)[...] = ((part21[...] + product(at(x, 2, 1)[...], at(x, 1, 1)[...])) * keep(2, 1)).astype(BF16)
+        at(s, 1, 1)[...] = ((part31[...] + product(at(x, 3, 1)[...], at(x, 1, 1)[...])) * keep(3, 1)).astype(BF16)
+        finish(2, 0, at(total, 0, 0)[...] + product(at(s, 0, 0, 1, 2)[...], at(x, 0, 0, 2, 1)[...]))
+        finish(2, 1, at(total, 0, 1)[...] + product(at(s, 0, 0, 1, 2)[...], at(x, 0, 1, 2, 1)[...]))
+        at(total, 0, 2)[...] += product(at(s, 0, 0, 1, 2)[...], at(x, 0, 2, 2, 1)[...])
+        at(total, 0, 3)[...] += product(at(s, 0, 1)[...], at(x, 1, 3)[...])
+        finish(3, 1, at(total, 1, 1)[...] + product(at(s, 1, 1)[...], at(x, 1, 1)[...]))
+        for col in (2, 3):
+            at(total, 1, col)[...] += product(at(s, 1, 1)[...], at(x, 1, col)[...])
+
+    def high_44():
+        arrived(odd, 0, 6, 7)
+        unpack_side(tiles.at[high, 0], at(x, 4, 4))
+        unpack(tiles.at[high, 2], lines.at[high], 0, at(x, 4, 4))
         value = partial[:, :B] + product(at(x, 2, 4, 2, 1)[...], at(x, 4, 4)[...])
         at(s, 0, 4)[...] = (value[:B] * keep(2, 4)).astype(BF16)
         partial[B:, :B] = value[B:]
@@ -199,55 +326,66 @@
             at(total, 0, col)[...] += product(at(s, 0, 4)[...], at(x, 4, col)[...])
         finish(2, 4, at(total, 0, 4)[...] + product(at(s, 0, 4)[...], at(x, 4, 4)[...]))
 
-    first_in_run = lax.axis_index("col") == 0
-    pl.when(first_in_run)(near_corner)
-
-    copies[0, 5].wait_recv()
-    unpack_side(low.at[3], at(x, 1, 1))
-    copies[0, 4].wait_recv()
-    unpack_side(low.at[2], at(x, 0, 0))
-    copies[0, 2].wait_recv()
-    at(x, 1, 0)[...] = at(x, 0, 1)[...].T
-    copies[0, 3].wait_recv()
-    copies[0, 1].wait_recv()
-    unpack(low.at[1], low_diagonals, 1, at(x, 1, 1))
-    square(2, 1, 0, 4)
-    square(3, 1, 1, 4)
-    copies[0, 0].wait_recv()
-    unpack(low.at[0], low_diagonals, 0, at(x, 0, 0))
-    square(2, 0, 0, 3)
-    finish(2, 0, at(total, 0, 0)[...] + product(at(s, 0, 0, 1, 2)[...], at(x, 0, 0, 2, 1)[...]))
-    finish(2, 1, at(total, 0, 1)[...] + product(at(s, 0, 0, 1, 2)[...], at(x, 0, 1, 2, 1)[...]))
-    at(total, 0, 2)[...] += product(at(s, 0, 0, 1, 2)[...], at(x, 0, 2, 2, 1)[...])
-    at(total, 0, 3)[...] += product(at(s, 0, 1)[...], at(x, 1, 3)[...])
-    finish(3, 1, at(total, 1, 1)[...] + product(at(s, 1, 1)[...], at(x, 1, 1)[...]))
-    for col in (2, 3):
-        at(total, 1, col)[...] += product(at(s, 1, 1)[...], at(x, 1, col)[...])
-
-    pl.when(jnp.logical_not(first_in_run))(near_corner)
-    for col in (2, 3):
-        finish(2, col, at(total, 0, col)[...])
-
-    copies[1, 2].wait_recv()
-    at(x, 5, 4)[...] = at(x, 4, 5)[...].T
-    value = partial[B:, :B] + product(at(x, 3, 5)[...], at(x, 5, 4)[...])
-    at(s, 1, 4)[...] = (value * keep(3, 4)).astype(BF16)
-    for col in (2, 3, 4, 5):
-        finish(3, col, at(total, 1, col)[...] + product(at(s, 1, 4)[...], at(x, 4, col)[...]))
-    value = partial[B:, B:] + product(at(x, 3, 4)[...], at(x, 4, 5)[...])
-    last_rows[...] = at(x, 5, 3, 1, 2)[...]
-    left[...] = at(x, 3, 5)[...]
-    copies[1, 5].wait_recv()
-    part_square[:, :H] = value[:, :H] + product(left[:, H:], last_side[...].T)
-    part_square[:, H:] = value[:, H:] + product(left[:, :H], last_side[...])
-    copies[1, 1].wait_recv()
-    for n in range(6):
-        copies[1, n].wait_send()
-
-    @pl.when(jnp.logical_not(last_in_run))
-    def _():
-        for n in range(6):
-            copies[0, n].wait_send()
+    def high_45():
+        arrived(odd, *STRIPS)
+        at(x, 4, 5)[...] = sides[high]
+        at(x, 5, 4)[...] = sides[high].T
+        last_rows[:, B:] = at(x, 5, 4)[...]
+        value = partial[B:, :B] + product(at(x, 3, 5)[...], at(x, 5, 4)[...])
+        at(s, 1, 4)[...] = (value * keep(3, 4)).astype(BF16)
+        for col in (2, 3):
+            at(total, 1, col)[...] += product(at(s, 1, 4)[...], at(x, 4, col)[...])
+        for col in (4, 5):
+            finish(3, col, at(total, 1, col)[...] + product(at(s, 1, 4)[...], at(x, 4, col)[...]))
+        arrived(odd, 1)
+        side = tiles[high, 1]
+        value = partial[B:, B:] + product(at(x, 3, 4)[...], at(x, 4, 5)[...])
+        part_square[:, :H] = value[:, :H] + product(left[:, H:], side.T)
+        part_square[:, H:] = value[:, H:] + product(left[:, :H], side)
+        last_side[...] = side
+
+    pass_on(jnp.logical_not(ends), STRIPS)
+    pl.when(odd)(low_01)
+    forward(6)
+    forward(7)
+    pl.when(odd)(low_00)
+    pl.when(even)(high_44)
+    forward(8)
+    pl.when(odd)(low_11)
+    pl.when(even)(high_45)
+    pass_on(ends, OTHERS)
+
+    @pl.when(odd)
+    def _():
+        high_44()
+        high_45()
+
+    @pl.when(even)
+    def _():
+        low_01()
+        low_00()
+        low_11()
+
+    for row, col in ((2, 2), (2, 3), (3, 2), (3, 3)):
+        finish(row, col, at(total, row - 2, col)[...])
+    arrived(odd, 8)
+    last_tile[...] = tiles[high, 3]
+    last_diagonals[...] = lines[high]
+
+    for n in range(PIECES):
+        direct[n].wait_send()
+        when(jnp.logical_not(spared))(onward[n].wait_send)
+    for condition, copies, pieces in (
+        (spared, aside, OTHERS),
+        (crossing, across, STRIPS),
+        (jnp.logical_and(relay, ends), relays, OTHERS),
+        (jnp.logical_and(relay, jnp.logical_not(ends)), relays, STRIPS),
+    ):
+
+        @when(condition)
+        def _():
+            for n in pieces:
+                copies[n].wait_send()
 
 
 def tail(occupancy, done, base, part_square, left, last_rows, last_side, last_tile, last_diagonals, out, corner, late, store_sem):
@@ -304,13 +442,13 @@
             pltpu.VMEM((OWN * B, 2 * B), F32),
             pltpu.VMEM((2, H, H), BF16),
             pltpu.VMEM((16, H // 2), BF16),
-            pltpu.VMEM((4, H, H), BF16),
-            pltpu.VMEM((16, H // 2), BF16),
-            pltpu.VMEM((2, H, H), BF16),
+            pltpu.VMEM((3, 4, H, H), BF16),
+            pltpu.VMEM((3, B, B), BF16),
+            pltpu.VMEM((3, 16, H // 2), BF16),
             pltpu.SMEM((OWN, SLOTS), jnp.int32),
             dma((OWN * SLOTS + 1,)),
-            dma((2, 6)),
-            dma((2, 6)),
+            dma((3, PIECES)),
+            dma((3, PIECES)),
             pltpu.SemaphoreType.REGULAR,
         ],
         compiler_params=pltpu.CompilerParams(

time: 54.4 us -> 49.2 us (0.904)
  Pallas kernels: 54.1 us -> 48.9 us
    pallas_call x1, Pallas kernels: 51.1 us -> 45.9 us  [on_device(): pl.pallas_call(kernel, out_shape=(pltpu.VMEM(band_blocks.shape, BF16), pl...]
where the time goes in v5:
time: 49.2 us; the launch traced here: 49.1 us
  Pallas kernels  48.9 us (99%)
    pallas_call x1, Pallas kernels, on_device(): pl.pallas_call(kernel, out_shape=(pltpu.VMEM(band_blocks.shape, BF16), pl...  45.9 us
    pallas_call x1, Pallas kernels, on_device(): pl.pallas_call(tail, out_shape=jax.ShapeDtypeStruct(band_blocks.shape, BF...  2.97 us

profile of v5, /device:TPU:0, one launch (start us, length us, event | category | flops | bytes accessed | tf_op | source)
XLA Modules:
  0.0 49.1 jit_solution(17238642046759678275)
XLA Ops:
  0.0 0.0 copy-start
  0.0 45.9 %step.1 = (bf16[2,5,512,512]{3,2,1,0:T(8,128)(2,1)S(1)}, f32[512,1536]{1,0:T(8,128)S(1)}, f32[512,512]{1,0:T(8,128)S(1)}, bf16[512,512]{1,0:T(8,128)(2,1)S(1)}, ...) custom-call(bf16[2,5,512,512]{3,2,1,0:T(8,128)(2,1)} %band.1, ...), custom_call_target="tpu_custom_call" | custom-call | tf_op jit(solution)/shard_map/step/pallas_call | solution.py:424
  45.9 0.0 copy-done
  45.9 3.0 %finish.1 = bf16[2,5,512,512]{3,2,1,0:T(8,128)(2,1)} custom-call(s32[2,5]{1,0:T(2,128)S(1)} %copy-done, bf16[2,5,512,512]{3,2,1,0:T(8,128)(2,1)S(1)} %get-tuple-element.13.done, f32[512,1536]{1,0:T(8,128)S(1)} %get-tuple-element.14.base, f32[512,512]{1,0:T(8,128)S(1)} %get-tuple-element.15.part_square, bf16[512,512]{1,0:T(8,128)(2,1)S(1)} %get-tuple-element.16.left, ...), custom_call_target="tpu_custom_call" | custom-call | tf_op jit(solution)/shard_map/finish/pallas_call | solution.py:459
Async XLA Ops:
  0.0 45.9 %copy-start = (s32[2,5]{1,0:T(2,128)S(1)}, s32[2,5]{1,0:T(2,128)}, u32[]{:S(2)}) copy-start(s32[2,5]{1,0:T(2,128)} %occupancy.1) | copy-start | bytes 124

commit v6 on v5

--- a/solution.py
+++ b/solution.py
@@ -1,3 +1,5 @@
+import functools
+
 import jax
 import jax.numpy as jnp
 from jax import lax
@@ -288,6 +290,13 @@
         else:
             done[row - 2, col - (row - 2)] = block.astype(BF16)
 
+    def gather(last_part, row, col, value):
+        value = at(total, row - 2, col)[...] + value
+        if last_part:
+            finish(row, col, value)
+        else:
+            at(total, row - 2, col)[...] = value
+
     def low_01():
         arrived(even, *STRIPS)
         at(x, 0, 1)[...] = sides[low]
@@ -301,7 +310,7 @@
         unpack(tiles.at[low, 2], lines.at[low], 0, at(x, 0, 0))
         at(s, 0, 0)[...] = ((part20[...] + product(at(x, 2, 0)[...], at(x, 0, 0)[...])) * keep(2, 0)).astype(BF16)
 
-    def low_11():
+    def low_11(last_part):
         arrived(even, 1, 8)
         unpack_side(tiles.at[low, 1], at(x, 1, 1))
         unpack(tiles.at[low, 3], lines.at[low], 1, at(x, 1, 1))
@@ -309,13 +318,13 @@
         at(s, 1, 1)[...] = ((part31[...] + product(at(x, 3, 1)[...], at(x, 1, 1)[...])) * keep(3, 1)).astype(BF16)
         finish(2, 0, at(total, 0, 0)[...] + product(at(s, 0, 0, 1, 2)[...], at(x, 0, 0, 2, 1)[...]))
         finish(2, 1, at(total, 0, 1)[...] + product(at(s, 0, 0, 1, 2)[...], at(x, 0, 1, 2, 1)[...]))
-        at(total, 0, 2)[...] += product(at(s, 0, 0, 1, 2)[...], at(x, 0, 2, 2, 1)[...])
-        at(total, 0, 3)[...] += product(at(s, 0, 1)[...], at(x, 1, 3)[...])
+        gather(last_part, 2, 2, product(at(s, 0, 0, 1, 2)[...], at(x, 0, 2, 2, 1)[...]))
+        gather(last_part, 2, 3, product(at(s, 0, 1)[...], at(x, 1, 3)[...]))
         finish(3, 1, at(total, 1, 1)[...] + product(at(s, 1, 1)[...], at(x, 1, 1)[...]))
         for col in (2, 3):
-            at(total, 1, col)[...] += product(at(s, 1, 1)[...], at(x, 1, col)[...])
-
-    def high_44():
+            gather(last_part, 3, col, product(at(s, 1, 1)[...], at(x, 1, col)[...]))
+
+    def high_44(last_part):
         arrived(odd, 0, 6, 7)
         unpack_side(tiles.at[high, 0], at(x, 4, 4))
         unpack(tiles.at[high, 2], lines.at[high], 0, at(x, 4, 4))
@@ -323,10 +332,10 @@
         at(s, 0, 4)[...] = (value[:B] * keep(2, 4)).astype(BF16)
         partial[B:, :B] = value[B:]
         for col in (2, 3):
-            at(total, 0, col)[...] += product(at(s, 0, 4)[...], at(x, 4, col)[...])
+            gather(last_part, 2, col, product(at(s, 0, 4)[...], at(x, 4, col)[...]))
         finish(2, 4, at(total, 0, 4)[...] + product(at(s, 0, 4)[...], at(x, 4, 4)[...]))
 
-    def high_45():
+    def high_45(last_part):
         arrived(odd, *STRIPS)
         at(x, 4, 5)[...] = sides[high]
         at(x, 5, 4)[...] = sides[high].T
@@ -334,7 +343,7 @@
         value = partial[B:, :B] + product(at(x, 3, 5)[...], at(x, 5, 4)[...])
         at(s, 1, 4)[...] = (value * keep(3, 4)).astype(BF16)
         for col in (2, 3):
-            at(total, 1, col)[...] += product(at(s, 1, 4)[...], at(x, 4, col)[...])
+            gather(last_part, 3, col, product(at(s, 1, 4)[...], at(x, 4, col)[...]))
         for col in (4, 5):
             finish(3, col, at(total, 1, col)[...] + product(at(s, 1, 4)[...], at(x, 4, col)[...]))
         arrived(odd, 1)
@@ -345,29 +354,29 @@
         last_side[...] = side
 
     pass_on(jnp.logical_not(ends), STRIPS)
+    pass_on(ends, OTHERS[:2])
     pl.when(odd)(low_01)
     forward(6)
     forward(7)
     pl.when(odd)(low_00)
-    pl.when(even)(high_44)
+    pl.when(even)(functools.partial(high_44, False))
     forward(8)
-    pl.when(odd)(low_11)
-    pl.when(even)(high_45)
-    pass_on(ends, OTHERS)
+    pass_on(last_in_run, OTHERS[2:])
+    pl.when(odd)(functools.partial(low_11, False))
+    pl.when(even)(functools.partial(high_45, False))
+    pass_on(first_in_run, OTHERS[2:])
 
     @pl.when(odd)
     def _():
-        high_44()
-        high_45()
+        high_44(True)
+        high_45(True)
 
     @pl.when(even)
     def _():
         low_01()
         low_00()
-        low_11()
-
-    for row, col in ((2, 2), (2, 3), (3, 2), (3, 3)):
-        finish(row, col, at(total, row - 2, col)[...])
+        low_11(True)
+
     arrived(odd, 8)
     last_tile[...] = tiles[high, 3]
     last_diagonals[...] = lines[high]

time: 49.2 us -> 47.8 us (0.972)
  Pallas kernels: 48.9 us -> 47.5 us
    pallas_call x1, Pallas kernels: 45.9 us -> 44.5 us  [on_device(): pl.pallas_call(kernel, out_shape=(pltpu.VMEM(band_blocks.shape, BF16), pl...]
where the time goes in v6:
time: 47.8 us; the launch traced here: 47.7 us
  Pallas kernels  47.5 us (99%)
    pallas_call x1, Pallas kernels, on_device(): pl.pallas_call(kernel, out_shape=(pltpu.VMEM(band_blocks.shape, BF16), pl...  44.5 us
    pallas_call x1, Pallas kernels, on_device(): pl.pallas_call(tail, out_shape=jax.ShapeDtypeStruct(band_blocks.shape, BF...  2.97 us

profile of v6, /device:TPU:0, one launch (start us, length us, event | category | flops | bytes accessed | tf_op | source)
XLA Modules:
  0.0 47.7 jit_solution(8106503858883888772)
XLA Ops:
  0.0 0.0 copy-start
  0.0 44.5 %step.1 = (bf16[2,5,512,512]{3,2,1,0:T(8,128)(2,1)S(1)}, f32[512,1536]{1,0:T(8,128)S(1)}, f32[512,512]{1,0:T(8,128)S(1)}, bf16[512,512]{1,0:T(8,128)(2,1)S(1)}, ...) custom-call(bf16[2,5,512,512]{3,2,1,0:T(8,128)(2,1)} %band.1, ...), custom_call_target="tpu_custom_call" | custom-call | tf_op jit(solution)/shard_map/step/pallas_call | solution.py:433
  44.5 0.0 copy-done
  44.5 3.0 %finish.1 = bf16[2,5,512,512]{3,2,1,0:T(8,128)(2,1)} custom-call(s32[2,5]{1,0:T(2,128)S(1)} %copy-done, bf16[2,5,512,512]{3,2,1,0:T(8,128)(2,1)S(1)} %get-tuple-element.13.done, f32[512,1536]{1,0:T(8,128)S(1)} %get-tuple-element.14.base, f32[512,512]{1,0:T(8,128)S(1)} %get-tuple-element.15.part_square, bf16[512,512]{1,0:T(8,128)(2,1)S(1)} %get-tuple-element.16.left, ...), custom_call_target="tpu_custom_call" | custom-call | tf_op jit(solution)/shard_map/finish/pallas_call | solution.py:468
Async XLA Ops:
  0.0 44.5 %copy-start = (s32[2,5]{1,0:T(2,128)S(1)}, s32[2,5]{1,0:T(2,128)}, u32[]{:S(2)}) copy-start(s32[2,5]{1,0:T(2,128)} %occupancy.1) | copy-start | bytes 124
